TPU v7x, 512 devices: a whole 4x8x8 slice. The times are simulated.
512 devices in a mesh: dp: 16 (over y, core), vocab: 32 (over x, z).
Axes of the slice: x: 4, y: 8, z: 8, core: 2. Of those that a mesh axis runs over, the one named last changes fastest.
Arguments:
- states: bfloat16 [8192, 2048], P('dp'), may hold values from -8 to 8
- head_weight: bfloat16 [2048, 65536], P('dp', 'vocab')
- targets: int32 [8192], P('dp'), may hold values from 0 to 65535
- positions: int32 [32, 256], P('dp'), may hold values from 0 to 255, each once within a row
- counts: int32 [32], P('dp'), may hold values from 1 to 48, 896 in all
- rate_num: int32 [32], P('dp'), may hold values from 64 to 1024
Outputs:
- mean_loss: float32 [], replicated
- grad_hidden: bfloat16 [8192, 2048], P('dp', 'vocab')
- grad_weight: float32 [2048, 65536], P('dp', 'vocab')
Inputs may be any that keep to these rules, and one draw needn't show every extreme that they name: Largest count is 48; the counts sum to 896. Each row is a permutation of the positions.
All inputs are finite; a program needn't handle non-finite values. No bound on the sum of `counts` on one device may be relied on, other than what follows from the above.
Results may differ from a plain program's by a relative error of at most 0.0044.
Values may be sent and summed in bfloat16 or wider, within the bound.
A program may use at most 64 MiB of HBM per device.

v0:
```python
import jax
import jax.numpy as jnp
from jax import lax
from jax.sharding import PartitionSpec as P

CAP = 48
RATE_DEN = 1024


def masked_rows(positions, counts, rate_num):
    seq_count, length = positions.shape
    slot_ids = jnp.arange(CAP, dtype=jnp.int32)
    is_live = slot_ids[None, :] < counts[:, None]
    row_index = (
        jnp.arange(seq_count, dtype=jnp.int32)[:, None] * length + positions[:, :CAP]
    ).reshape(-1)
    row_weight = jnp.where(is_live, RATE_DEN / rate_num[:, None].astype(jnp.float32), 0.0).reshape(
        -1
    )
    return (row_index, row_weight)


def local(states, head_weight, targets, positions, counts, rate_num):
    row_index, row_weight = masked_rows(positions, counts, rate_num)
    chosen = states[row_index]
    labels = targets[row_index]
    weight_full = lax.all_gather(head_weight, "dp", axis=0, tiled=True)
    vocab_width = weight_full.shape[1]
    logits = jnp.dot(chosen, weight_full, preferred_element_type=jnp.float32)
    local_ids = labels - lax.axis_index("vocab") * vocab_width
    is_target = jnp.arange(vocab_width, dtype=jnp.int32)[None, :] == local_ids[:, None]
    target_part = jnp.sum(jnp.where(is_target, logits, 0.0), axis=1)
    row_high = lax.pmax(jnp.max(logits, axis=1), "vocab")
    local_total = jnp.sum(jnp.exp(logits - row_high[:, None]), axis=1)
    exp_total, target_logit = lax.psum((local_total, target_part), "vocab")
    log_total = row_high + jnp.log(exp_total)
    token_count = positions.shape[0] * lax.axis_size("dp") * positions.shape[1]
    mean_loss = lax.psum(jnp.sum(row_weight * (log_total - target_logit)), "dp") / token_count
    row_probs = jnp.exp(logits - log_total[:, None])
    grad_logits = (row_weight[:, None] * (row_probs - is_target.astype(jnp.float32))).astype(
        jnp.bfloat16
    )
    row_grads = lax.dot_general(
        grad_logits, weight_full, (((1,), (1,)), ((), ())), preferred_element_type=jnp.float32
    )
    share_width = row_grads.shape[1] // lax.axis_size("vocab")
    summed = lax.psum(row_grads, "vocab")
    grad_share = lax.dynamic_slice_in_dim(
        summed, lax.axis_index("vocab") * share_width, share_width, 1
    )
    grad_hidden = (
        jnp.zeros((states.shape[0], share_width), jnp.bfloat16)
        .at[row_index]
        .set(grad_share.astype(jnp.bfloat16))
    )
    feature_cols = lax.all_to_all(chosen, "dp", split_axis=1, concat_axis=0, tiled=True)
    grad_weight = lax.dot_general(
        feature_cols,
        lax.all_gather(grad_logits, "dp", axis=0, tiled=True),
        (((0,), (0,)), ((), ())),
        preferred_element_type=jnp.float32,
    )
    return (mean_loss, grad_hidden, grad_weight)


def solution(mesh):
    return jax.shard_map(
        local,
        mesh=mesh,
        in_specs=(P("dp", None), P("dp", "vocab"), P("dp"), P("dp", None), P("dp"), P("dp")),
        out_specs=(P(), P("dp", "vocab"), P("dp", "vocab")),
        check_vma=False,
    )
```

profile of v0, /device:TPU:1, one launch (start us, length us, event | category | flops | bytes accessed | tf_op | source)
XLA Modules:
  0.0 431.8 jit_solution(57700845239722556)
XLA Ops:
  7.2 0.7 all-gather.3.cloned.1.call-update
  8.0 0.7 convert_divide_fusion
  8.6 0.7 compare_select_fusion.1
  9.4 0.1 select_n.32
  9.4 0.7 slice_add_fusion
  10.3 1.6 gather_fusion.1
  11.9 0.8 gather_fusion
  12.8 61.5 %all-gather.3.cloned.1.call-done = bf16[2048,2048]{1,0:T(8,128)(2,1)} async-done(((bf16[128,2048]{1,0:T(8,128)(2,1)}), bf16[2048,2048]{1,0:T(8,128)(2,1)}) %all-gather.3.cloned.1.call-update) | async-done | bytes 8388624 | tf_op jit(solution)/shard_map/all_gather | solution.py:27
  74.3 5.0 %fusion.3 = (f32[96]{0:T(128)S(1)}, f32[96,2048]{1,0:T(8,128)S(1)}) fusion(bf16[96,2048]{1,0:T(8,128)(2,1)S(1)} %gather_fusion, bf16[2048,2048]{1,0:T(8,128)(2,1)} %all-gather.3.cloned.1.call-done), kind=kOutput, calls=%fused_computation.21 | convolution fusion | flops 805502848 | bytes 9568640 | tf_op jit(solution)/shard_map/dot_general | solution.py:29
  79.3 61.8 %pmax.7 = f32[96]{0:T(128)S(1)} all-reduce(f32[96]{0:T(128)S(1)} %get-tuple-element.10), channel_id=1, replica_groups=mesh['dp'=16,'vocab'=32] {'vocab'}, use_global_device_ids=true, to_apply=%region_1.2 | all-reduce | flops 96 | bytes 768 | tf_op jit(solution)/shard_map/pmax | solution.py:33
  141.1 0.4 select_reduce_fusion
  141.4 55.7 %psum.28 = f32[96]{0:T(128)S(1)} all-reduce(f32[96]{0:T(128)S(1)} %get-tuple-element.7), channel_id=1, replica_groups=mesh['dp'=16,'vocab'=32] {'vocab'}, use_global_device_ids=true, to_apply=%region_3.4 | all-reduce | flops 96 | bytes 768 | tf_op jit(solution)/shard_map/psum | solution.py:35
  197.2 1.2 multiply_convert_fusion
  198.4 0.8 copy_bitcast_fusion
  199.2 32.5 %all-to-all-start = ((bf16[96,16,128]{2,0,1:T(8,128)(2,1)}), bf16[96,16,128]{2,0,1:T(8,128)(2,1)S(1)}, u32[]{:S(2)}, u32[]{:S(2)}) async-start(bf16[96,16,128]{2,0,1:T(8,128)(2,1)} %copy_bitcast_fusion), calls=%async_computation | async-start | bytes 786432 | tf_op jit(solution)/shard_map/all_to_all | solution.py:56
  231.8 6.1 %fusion.4 = f32[96,2048]{0,1:T(8,128)S(1)} fusion(bf16[96,2048]{1,0:T(8,128)(2,1)} %multiply_convert_fusion, bf16[2048,2048]{1,0:T(8,128)(2,1)} %all-gather.3.cloned.1.call-done), kind=kOutput, calls=%fused_computation.22 | convolution fusion | flops 805306368 | bytes 9568256 | tf_op jit(solution)/shard_map/dot_general | solution.py:43
  237.9 127.3 %all-reduce.2 = (f32[96]{0:T(128)}, bf16[96,2048]{0,1:T(8,128)(2,1)}) all-reduce(f32[96]{0:T(128)S(1)} %get-tuple-element.6, f32[96,2048]{0,1:T(8,128)S(1)} %fusion.4), channel_id=1, replica_groups=mesh['dp'=16,'vocab'=32] {'vocab'}, use_global_device_ids=true, to_apply=%region_5.6 | all-reduce | flops 196704 | bytes 1180416 | tf_op jit(solution)/shard_map/psum | solution.py:35
  365.2 1.3 multiply_reduce_fusion
  366.5 49.5 %psum.30 = f32[]{:T(128)} all-reduce(f32[]{:T(128)} %multiply_reduce_fusion), channel_id=1, replica_groups=mesh['dp'=16,'vocab'=32] {'dp'}, use_global_device_ids=true, to_apply=%region_7.8 | all-reduce | flops 1 | bytes 8 | tf_op jit(solution)/shard_map/psum | solution.py:38
  416.0 0.7 dynamic-slice_convert_fusion
  416.7 0.1 copy.9
  416.8 0.9 scatter_custom_fusion
  417.7 0.7 copy.11
  419.1 4.8 %fusion.5 = f32[128,2048]{1,0:T(8,128)} fusion(bf16[1536,128]{1,0:T(8,128)(2,1)S(1)} %bitcast.17, bf16[1536,2048]{1,0:T(8,128)(2,1)} %all-gather.5.cloned.1.call-done), kind=kOutput, calls=%fused_computation.23 | convolution fusion | flops 805306368 | bytes 7733248 | tf_op jit(solution)/shard_map/dot_general | solution.py:57
  (13 shorter events, 0.2 us)
Async XLA Ops:
  7.2 4.8 %copy-start = (bf16[512,2048]{1,0:T(8,128)(2,1)S(1)}, bf16[512,2048]{1,0:T(8,128)(2,1)}, u32[]{:S(2)}) copy-start(bf16[512,2048]{1,0:T(8,128)(2,1)} %param.6) | copy-start | bytes 6291460
  7.2 67.1 %all-gather.3.cloned.1.call-start = ((), (), s32[]{:S(2)}) async-start(), calls=%async_computation.1 | async-start | bytes 8912896 | tf_op jit(solution)/shard_map/all_gather | solution.py:27
  7.9 411.2 %all-gather.5.cloned.1.call-start = ((), (), s32[]{:S(2)}) async-start(), calls=%async_computation.2 | async-start | bytes 6684672 | tf_op jit(solution)/shard_map/all_gather | solution.py:59
  199.2 219.8 %all-to-all-start = ((bf16[96,16,128]{2,0,1:T(8,128)(2,1)}), bf16[96,16,128]{2,0,1:T(8,128)(2,1)S(1)}, u32[]{:S(2)}, u32[]{:S(2)}) async-start(bf16[96,16,128]{2,0,1:T(8,128)(2,1)} %copy_bitcast_fusion), calls=%async_computation | async-start | bytes 786432 | tf_op jit(solution)/shard_map/all_to_all | solution.py:56
Sparse Core Ops, SparseCore 0:
  10.1 64.1 all-gather.2
  198.5 76.9 all-gather.4
where the time goes:
time: 432 us
  blocking collectives  294 us (68%)
  waiting for transfers between devices  62.2 us (14%)
  starting transfers between devices  32.6 us (8%)
  matrix products  15.9 us (4%)
  between operations  15.9 us (4%)
  local copies, waits for them, and re-layouts  5.91 us (1%)
  other arithmetic  5 us (1%)
    psum x2, blocking collectives, local(): exp_total, target_logit = lax.psum((local_total, target_part), 'vocab')  183 us
    pmax x1, blocking collectives, local(): row_high = lax.pmax(jnp.max(logits, axis=1), 'vocab')  61.8 us
    all_gather x1, waiting for transfers between devices, local(): weight_full = lax.all_gather(head_weight, 'dp', axis=0, tiled=True)  61.5 us
    psum x1, blocking collectives, local(): lax.psum(jnp.sum(row_weight * (log_total - target_logit)), 'dp')  49.5 us
    all_to_all x1, starting transfers between devices, local(): lax.all_to_all(chosen, 'dp', split_axis=1, concat_axis=0, tiled=True)  32.5 us
  transfers between devices with their start and end apart: 3, of which 1 were waited for; matrix products, arithmetic and copies ran while one was open for 4% of the time, Pallas kernels for 0%

commit v1 on v0

v1 whole, which is shorter than its diff:
```python
import functools

import jax
import jax.numpy as jnp
from jax import lax
from jax.experimental import pallas as pl
from jax.experimental.pallas import tpu as pltpu
from jax.sharding import PartitionSpec as P

MESH = pl.DeviceIdType.MESH
F32 = jnp.float32
BF16 = jnp.bfloat16

CAP = 48
LIVE = 896
RATE_DEN = 1024
NX = 4
META = 16


def nn(a, b):
    return lax.dot_general(a, b, (((1,), (0,)), ((), ())), preferred_element_type=F32)


def nt(a, b):
    return lax.dot_general(a, b, (((1,), (1,)), ((), ())), preferred_element_type=F32)


def tn(a, b):
    return lax.dot_general(a, b, (((0,), (0,)), ((), ())), preferred_element_type=F32)


def iota(shape, dim):
    return lax.broadcasted_iota(jnp.int32, shape, dim)


def kernel(
    cfg,
    counts_ref,
    rate_ref,
    pos_ref,
    tgt_ref,
    states_ref,
    w_ref,
    loss_ref,
    gh_ref,
    gw_ref,
    s_buf,
    pmt,
    blocks,
    wc,
    xg,
    e_buf,
    xd,
    rank_buf,
    meta,
    qun,
    lse_y,
    lse_x,
    lse_z,
    stat,
    ght,
    red,
    fin,
    u_buf,
    s_sem,
    a_send,
    a_recv,
    w_send,
    w_recv,
    wf_send,
    wf_recv,
    core_send,
    core_recv,
    x_send,
    x_recv,
    zr_send,
    zr_recv,
    e_send,
    e_recv,
    ef_send,
    ef_recv,
    ly_send,
    ly_recv,
    lx_send,
    lx_recv,
    lz_send,
    lz_recv,
    r_send,
    r_recv,
    u_send,
    u_recv,
):
    ny, nx, nz, vw, slots, tokens, seq, all_tokens = cfg
    ndp, nch = 2 * ny, nx * nz
    rc = LIVE // 2
    rh = rc // 2
    width = stat.shape[2]
    dg = 128 // (nch // 2)

    dp = lax.axis_index("dp")
    vo = lax.axis_index("vocab")
    y, c = dp // 2, dp % 2
    x, z = vo // nz, vo % nz
    here = c * ny + y
    piece = z * nx + x
    m, h = piece // 2, piece % 2
    pending = []

    def rem(src, dst, send, recv, device):
        return pltpu.make_async_remote_copy(
            src_ref=src,
            dst_ref=dst,
            send_sem=send,
            recv_sem=recv,
            device_id=device,
            device_id_type=MESH,
        )

    def go(src, dst, send, recv, device):
        copy = rem(src, dst, send, recv, device)
        copy.start()
        pending.append(copy)

    def arrived(dst, send, recv):
        rem(dst, dst, send, recv, (dp, vo)).wait_recv()

    def in_column(yy):
        return (2 * yy + c, vo)

    sibling = (2 * y + 1 - c, vo)
    peer_x = lambda xx: (dp, xx * nz + z)
    peer_z = lambda zz: (dp, x * nz + zz)

    states_copy = pltpu.make_async_copy(
        states_ref.at[:, pl.ds(pl.multiple_of(m * 128, 128), 128)], s_buf, s_sem
    )
    states_copy.start()

    barrier = pltpu.get_barrier_semaphore()
    q = vo
    g, half_q = q // 2, q % 2
    target_vo = 2 * dp + g // (nch // 4)
    src_dp, src_q0 = vo // 2, (nch // 2) * (vo % 2)

    def signal(device):
        pl.semaphore_signal(barrier, inc=1, device_id=device, device_id_type=MESH)

    for k in range(1, ny):
        signal(in_column((y + k) % ny))
    signal(sibling)

    def signal_plane(k, carry):
        signal((dp, (vo + k) % nch))
        return carry

    lax.fori_loop(1, nch, signal_plane, 0)

    def signal_source(t, carry):
        to_self = (src_dp == dp) & (src_q0 + t == vo)

        @pl.when(jnp.logical_not(to_self))
        def _():
            signal((src_dp, src_q0 + t))

        return carry

    lax.fori_loop(0, nch // 2, signal_source, 0)

    lane = iota((8, 128), 1)
    pos0 = jnp.broadcast_to(pos_ref[0:1, 0:128], (8, 128))
    pos1 = jnp.broadcast_to(pos_ref[1:2, 0:128], (8, 128))
    pos1 = pltpu.roll(pos1, CAP, 1)
    tok = jnp.where(lane < CAP, pos0, jnp.where(lane < 2 * CAP, seq + pos1, -1))[0:1]
    pmt[...] = jnp.where(iota((tokens, 128), 0) == tok, 1.0, 0.0).astype(BF16)
    targets = tgt_ref[...]
    row16 = iota((META, tokens), 0)
    parts = jnp.where(
        row16 == 0,
        jnp.right_shift(targets, 8).astype(F32),
        jnp.where(row16 == 1, jnp.bitwise_and(targets, 255).astype(F32), 0.0),
    ).astype(BF16)
    label_rows = nn(parts, pmt[...])
    lane16 = iota((META, 128), 1)
    row16 = iota((META, 128), 0)

    def per_slot(first, second):
        return jnp.where(
            lane16 < CAP, first, jnp.where(lane16 < 2 * CAP, second, 0)
        ).astype(F32)

    r0, r1 = rate_ref[0], rate_ref[1]
    own_meta = jnp.where(row16 == 2, per_slot(jnp.right_shift(r0, 8), jnp.right_shift(r1, 8)), label_rows)
    own_meta = jnp.where(row16 == 3, per_slot(jnp.bitwise_and(r0, 255), jnp.bitwise_and(r1, 255)), own_meta)
    own_meta = jnp.where(row16 == 4, per_slot(counts_ref[0], counts_ref[1]), own_meta)
    states_copy.wait()
    chosen = tn(pmt[...], s_buf[...])
    blocks[c, y, 0:slots, :] = chosen[0:slots].astype(BF16)
    blocks[c, y, slots : slots + META, :] = own_meta.astype(BF16)

    n_to = (ny - 1) + 1 + (nch - 1)
    sends_self = jnp.where(target_vo == vo, 1, 0)
    pl.semaphore_wait(barrier, n_to + ndp - sends_self)

    for k in range(1, ny):
        go(blocks.at[c, y], blocks.at[c, y], a_send.at[k], a_recv.at[k], in_column((y + k) % ny))
    for k in range(1, ny):
        yy = (y + k) % ny
        go(
            w_ref.at[:, pl.ds(pl.multiple_of(yy * vw, vw), vw)],
            wc.at[dp],
            w_send.at[k],
            w_recv.at[k],
            in_column(yy),
        )
    wc[dp] = w_ref[:, pl.ds(pl.multiple_of(y * vw, vw), vw)]
    go(wc.at[dp], wc.at[dp], wf_send.at[0], wf_recv.at[0], sibling)
    for k in range(1, ny):
        arrived(blocks.at[c, (y + ny - k) % ny], a_send.at[k], a_recv.at[k])
    go(blocks.at[c], blocks.at[c], core_send.at[0], core_recv.at[0], sibling)
    arrived(blocks.at[1 - c], core_send.at[0], core_recv.at[0])

    all_meta = blocks[:, :, slots : slots + META, :].astype(F32).reshape(ndp, META, 128)
    count_rows = jnp.sum(
        jnp.where(iota((ndp, META, 128), 1) == 4, all_meta, 0.0), axis=1
    )
    first, second = count_rows[:, 0:1], count_rows[:, CAP : CAP + 1]
    in_all = jnp.broadcast_to(first + second, (ndp, 128)).astype(BF16)

    def order(v):
        return 2 * (v % ny) + v // ny

    earlier = jnp.where(
        order(iota((ndp, ndp), 1)) < order(iota((ndp, ndp), 0)), 1.0, 0.0
    ).astype(BF16)
    offset = nn(earlier, in_all)
    lanes = iota((ndp, 128), 1).astype(F32)
    in_first = lanes < CAP
    place = jnp.where(in_first, lanes, lanes - CAP + first)
    bound = jnp.where(in_first, first, second)
    local_place = jnp.where(in_first, lanes, lanes - CAP)
    live = (local_place < bound) & (lanes < 2 * CAP)
    rank_buf[...] = jnp.where(live, offset + place, -1.0)

    def one_hot(start, rows, a):
        names = iota((rows, 128), 0) + start
        return jnp.where(names.astype(F32) == rank_buf[a : a + 1, :], 1.0, 0.0).astype(BF16)

    acc = jnp.zeros((rh, 128), F32)
    for a in range(ndp):
        pick = one_hot(c * rc + h * rh, rh, a)
        acc += nn(pick[:, 0:slots], blocks[a // ny, a % ny, 0:slots, :])
    xg[piece] = acc.astype(BF16)
    for k in range(1, nx):
        go(xg.at[piece], xg.at[piece], x_send.at[k], x_recv.at[k], peer_x((x + k) % nx))

    def metas(core):
        total = jnp.zeros((rc, META), F32)
        for a in range(ndp):
            total += nt(one_hot(core * rc, rc, a), blocks[a // ny, a % ny, slots : slots + META, :])
        meta[core] = total

    def ring(n, me, block, subs, send, recv, device):
        last = n // 2 - 1

        def moves(step):
            for sub in range(subs):
                for way in (0, 1):
                    if step < last or (sub < subs // 2) == (way == 0):
                        yield way, sub

        def start(step, way, sub):
            origin = (me + n - step) % n if way == 0 else (me + step) % n
            to = (me + 1) % n if way == 0 else (me + n - 1) % n
            ref = block(origin, sub)
            go(ref, ref, send.at[way, step, sub], recv.at[way, step, sub], device(to))

        def wait(step, way, sub):
            origin = (me + n - 1 - step) % n if way == 0 else (me + 1 + step) % n
            ref = block(origin, sub)
            arrived(ref, send.at[way, step, sub], recv.at[way, step, sub])
            return origin

        return last, moves, start, wait

    x_last, x_moves, x_start, x_wait = ring(
        nz, z, lambda o, sub: xg.at[o * nx + sub], nx, zr_send, zr_recv, peer_z
    )

    metas(0)
    for k in range(1, nx):
        arrived(xg.at[z * nx + (x + nx - k) % nx], x_send.at[k], x_recv.at[k])
    for way, sub in x_moves(0):
        x_start(0, way, sub)

    metas(1)
    for a in range(ndp):
        qun[:, a * 128 : (a + 1) * 128] = one_hot(half_q * rc, rc, a)

    def w_arrive(k):
        from_dp = 2 * ((y + ny - k) % ny) + c
        arrived(wc.at[from_dp], w_send.at[k], w_recv.at[k])
        go(wc.at[from_dp], wc.at[from_dp], wf_send.at[k], wf_recv.at[k], sibling)

    w_order = sorted(range(1, ny), key=lambda k: min(k, ny - k))
    for step in range(x_last + 1):
        following = set(x_moves(step + 1)) if step < x_last else set()
        for way, sub in x_moves(step):
            x_wait(step, way, sub)
            if (way, sub) in following:
                x_start(step + 1, way, sub)
        take = len(w_order) if step == x_last else 2
        for k in w_order[:take]:
            w_arrive(k)
        w_order = w_order[take:]
    for k in range(ny):
        from_dp = 2 * ((y + ny - k) % ny) + 1 - c
        arrived(wc.at[from_dp], wf_send.at[k], wf_recv.at[k])

    logits = jnp.zeros((rc, vw), F32)
    for mm in range(ndp):
        rows = xg[2 * mm : 2 * mm + 2].reshape(rc, 128)
        logits += nn(rows, wc[mm])
    high = jnp.max(logits, axis=1, keepdims=True)
    powers = jnp.exp(logits - high)
    sums = jnp.sum(powers, axis=1, keepdims=True)
    lse = high + jnp.log(sums)
    own_part = powers * (1.0 / sums)
    for sub in range(2):
        e_buf[c, y, sub] = own_part[sub * rh : (sub + 1) * rh].astype(BF16)

    def label_of(core):
        rows = meta[core]
        return (rows[:, 0:1] * 256.0 + rows[:, 1:2]).astype(jnp.int32)

    def weight_of(core):
        rows = meta[core]
        return RATE_DEN / (rows[:, 2:3] * 256.0 + rows[:, 3:4])

    labels, weights = label_of(c), weight_of(c)
    hit = iota((rc, vw), 1) == labels - (vo * (vw * ny) + y * vw)
    of_targets = jnp.sum(jnp.sum(jnp.where(hit, logits * weights, 0.0), axis=1, keepdims=True), axis=0, keepdims=True)

    lse_row = jnp.transpose(jnp.broadcast_to(lse, (rc, 128)))[0:1]
    lse_y[y, :, 0:rc] = lse_row
    lse_y[y, :, rc:width] = jnp.broadcast_to(of_targets, (1, width - rc))

    for k in range(1, ny):
        go(lse_y.at[y], lse_y.at[y], ly_send.at[k], ly_recv.at[k], in_column((y + k) % ny))

    e_last, e_moves, e_start, e_wait = ring(
        ny, y, lambda o, sub: e_buf.at[c, o, sub], 2, e_send, e_recv, in_column
    )
    for way, sub in e_moves(0):
        e_start(0, way, sub)

    def share(offset, sub):
        o = (y + offset) % ny
        ref = e_buf.at[c, o, sub]
        go(ref, ref, ef_send.at[offset, sub], ef_recv.at[offset, sub], sibling)

    def shared(offset, sub):
        o = (y + offset) % ny
        arrived(e_buf.at[1 - c, o, sub], ef_send.at[offset, sub], ef_recv.at[offset, sub])

    share(0, 0)
    share(0, 1)
    go(xg.at[pl.ds(2 * (dp + 1 - 2 * c), 2)], xd.at[c], core_send.at[1], core_recv.at[1], sibling)
    xd[c] = xg[pl.ds(2 * dp, 2)]

    in_rows = iota((1, width), 1) < rc

    def combine(ref, n):
        rows = [ref[i] for i in range(n)]
        top = functools.reduce(jnp.maximum, rows)
        exps = functools.reduce(jnp.add, [jnp.exp(r - top) for r in rows])
        plain = functools.reduce(jnp.add, rows)
        return jnp.where(in_rows, top + jnp.log(exps), plain)

    for k in range(1, ny):
        arrived(lse_y.at[(y + ny - k) % ny], ly_send.at[k], ly_recv.at[k])
    lse_x[x] = combine(lse_y, ny)
    for k in range(1, nx):
        go(lse_x.at[x], lse_x.at[x], lx_send.at[k], lx_recv.at[k], peer_x((x + k) % nx))
    for k in range(1, nx):
        arrived(lse_x.at[(x + nx - k) % nx], lx_send.at[k], lx_recv.at[k])
    lse_z[z] = combine(lse_x, nx)
    for k in range(1, nz):
        go(lse_z.at[z], lse_z.at[z], lz_send.at[k], lz_recv.at[k], peer_z((z + k) % nz))
    for k in range(1, nz):
        arrived(lse_z.at[(z + nz - k) % nz], lz_send.at[k], lz_recv.at[k])
    log_total = combine(lse_z, nz)
    for k in range(ny):
        stat[c, k : k + 1, :] = lse_y[(y + k) % ny]
    stat[c, ny : ny + 1, :] = log_total
    go(stat.at[c], stat.at[c], core_send.at[2], core_recv.at[2], sibling)

    arrived(xd.at[1 - c], core_send.at[1], core_recv.at[1])
    features = [jnp.transpose(xd[core].reshape(rc, 128)) for core in range(2)]
    arrived(stat.at[1 - c], core_send.at[2], core_recv.at[2])

    scales, label_cols, weight_cols = [], [], []
    loss = jnp.zeros((1, 1), F32)
    for core in range(2):
        rows = stat[core]
        cols = jnp.transpose(rows)[0:rc]
        label_cols.append(label_of(core))
        weight_cols.append(weight_of(core))
        total_col = cols[:, ny : ny + 1]
        scales.append(weight_cols[core] * jnp.exp(cols - total_col))
        loss += jnp.sum(weight_cols[core] * total_col, axis=0, keepdims=True)
        loss -= rows[ny : ny + 1, rc : rc + 1]
    loss_ref[...] = loss * (1.0 / all_tokens)

    def process(offset, fresh):
        o = (y + offset) % ny
        columns = pl.ds(pl.multiple_of(o * vw, vw), vw)
        grad = jnp.zeros((128, vw), F32)
        for core in range(2):
            part = e_buf[core, o].reshape(rc, vw).astype(F32)
            hit = iota((rc, vw), 1) == label_cols[core] - (vo * (vw * ny) + o * vw)
            scaled = part * scales[core][:, offset : offset + 1]
            g_logits = jnp.where(hit, scaled - weight_cols[core], scaled).astype(BF16)
            grad += nn(features[core], g_logits)
            term = nt(w_ref[:, columns], g_logits)
            if fresh:
                ght[core] = term
            else:
                ght[core] += term
        gw_ref[:, columns] = grad

    shared(0, 0)
    shared(0, 1)
    process(0, True)
    for step in range(e_last + 1):
        following = set(e_moves(step + 1)) if step < e_last else set()
        came = set()
        for way, sub in e_moves(step):
            e_wait(step, way, sub)
            if (way, sub) in following:
                e_start(step + 1, way, sub)
            offset = (ny - 1 - step) if way == 0 else 1 + step
            share(offset, sub)
            came.add(offset)
        for offset in sorted(came):
            shared(offset, 0)
            shared(offset, 1)
            process(offset, False)

    def piece_of(qq):
        return ght.at[qq % 2, pl.ds(pl.multiple_of((qq // 2) * dg, dg), dg), :]

    def send_piece(k, carry):
        to = (vo + k) % nch
        rem(piece_of(to), red.at[vo], r_send.at[k], r_recv.at[k], (dp, to)).start()
        return carry

    lax.fori_loop(1, nch, send_piece, 0)
    red[vo] = ght[half_q, pl.ds(pl.multiple_of(g * dg, dg), dg), :]

    def take_piece(k, carry):
        frm = (vo + nch - k) % nch
        arrived(red.at[frm], r_send.at[k], r_recv.at[k])
        return carry

    lax.fori_loop(1, nch, take_piece, 0)
    final = jnp.sum(red[...], axis=0)
    in_slots = nn(final.astype(BF16), qun[...])
    for a in range(ndp):
        fin[a] = in_slots[:, a * 128 : (a + 1) * 128]
    slot = vo % (nch // 2)

    def is_self(a):
        return (target_vo == vo) & (a == here)

    def send_final(a, carry):
        to = (2 * (a % ny) + a // ny, target_vo)

        @pl.when(jnp.logical_not(is_self(a)))
        def _():
            rem(fin.at[a], u_buf.at[slot], u_send.at[a], u_recv.at[slot], to).start()

        return carry

    lax.fori_loop(0, ndp, send_final, 0)

    @pl.when(target_vo == vo)
    def _():
        u_buf[slot] = fin[here]

    def take_final(t, carry):
        from_self = (src_dp == dp) & (src_q0 + t == vo)

        @pl.when(jnp.logical_not(from_self))
        def _():
            arrived(u_buf.at[t], u_send.at[0], u_recv.at[t])

        return carry

    lax.fori_loop(0, nch // 2, take_final, 0)
    pieces = [u_buf[2 * t] + u_buf[2 * t + 1] for t in range(nch // 4)]
    columns = jnp.concatenate(pieces, axis=0).astype(BF16)
    gh_ref[...] = nt(pmt[...], columns).astype(BF16)

    for copy in pending:
        copy.wait_send()

    def sent_piece(k, carry):
        to = (vo + k) % nch
        rem(piece_of(to), red.at[vo], r_send.at[k], r_recv.at[k], (dp, to)).wait_send()
        return carry

    lax.fori_loop(1, nch, sent_piece, 0)

    def sent_final(a, carry):
        to = (2 * (a % ny) + a // ny, target_vo)

        @pl.when(jnp.logical_not(is_self(a)))
        def _():
            rem(fin.at[a], u_buf.at[slot], u_send.at[a], u_recv.at[slot], to).wait_send()

        return carry

    lax.fori_loop(0, ndp, sent_final, 0)


def local(states, head_weight, targets, positions, counts, rate_num):
    ndp = lax.axis_size("dp")
    nch = lax.axis_size("vocab")
    ny, nx, nz = ndp // 2, NX, nch // NX
    tokens, d = states.shape
    vw = head_weight.shape[1] // ny
    seqs, seq = positions.shape
    slots = seqs * CAP
    rc = LIVE // 2
    width = -(-(rc + 1) // 128) * 128
    dg = 128 // (nch // 2)
    stat_rows = -(-(ny + 1) // 8) * 8
    cfg = (ny, nx, nz, vw, slots, tokens, seq, ndp * tokens)
    dma = pltpu.SemaphoreType.DMA
    scratch = [
        pltpu.VMEM((tokens, 128), BF16),
        pltpu.VMEM((tokens, 128), BF16),
        pltpu.VMEM((2, ny, slots + META, 128), BF16),
        pltpu.VMEM((ndp, 128, vw), BF16),
        pltpu.VMEM((nch, rc // 2, 128), BF16),
        pltpu.VMEM((2, ny, 2, rc // 2, vw), BF16),
        pltpu.VMEM((2, 2, rc // 2, 128), BF16),
        pltpu.VMEM((ndp, 128), F32),
        pltpu.VMEM((2, rc, META), F32),
        pltpu.VMEM((rc, ndp * 128), BF16),
        pltpu.VMEM((ny, 1, width), F32),
        pltpu.VMEM((nx, 1, width), F32),
        pltpu.VMEM((nz, 1, width), F32),
        pltpu.VMEM((2, stat_rows, width), F32),
        pltpu.VMEM((2, 128, rc), F32),
        pltpu.VMEM((nch, dg, rc), F32),
        pltpu.VMEM((ndp, dg, 128), F32),
        pltpu.VMEM((nch // 2, dg, 128), F32),
        dma,
        dma((ny,)),
        dma((ny,)),
        dma((ny,)),
        dma((ny,)),
        dma((ny,)),
        dma((ny,)),
        dma((3,)),
        dma((3,)),
        dma((nx,)),
        dma((nx,)),
        dma((2, nz // 2, nx)),
        dma((2, nz // 2, nx)),
        dma((2, ny // 2, 2)),
        dma((2, ny // 2, 2)),
        dma((ny, 2)),
        dma((ny, 2)),
        dma((ny,)),
        dma((ny,)),
        dma((nx,)),
        dma((nx,)),
        dma((nz,)),
        dma((nz,)),
        dma((nch,)),
        dma((nch,)),
        dma((ndp,)),
        dma((nch // 2,)),
    ]
    vmem = pl.BlockSpec(memory_space=pltpu.VMEM)
    smem = pl.BlockSpec(memory_space=pltpu.SMEM)
    loss, grad_hidden, grad_weight = pl.pallas_call(
        functools.partial(kernel, cfg),
        out_shape=(
            jax.ShapeDtypeStruct((1, 1), F32),
            jax.ShapeDtypeStruct((tokens, d // nch), BF16),
            jax.ShapeDtypeStruct(head_weight.shape, F32),
        ),
        in_specs=[smem, smem, vmem, vmem, pl.BlockSpec(memory_space=pl.ANY), vmem],
        out_specs=(vmem, vmem, vmem),
        scratch_shapes=scratch,
        compiler_params=pltpu.CompilerParams(
            collective_id=0, has_side_effects=True, vmem_limit_bytes=48 * 1024 * 1024
        ),
    )(counts, rate_num, positions, targets.reshape(1, tokens), states, head_weight)
    return loss[0, 0], grad_hidden, grad_weight


def solution(mesh):
    return jax.shard_map(
        local,
        mesh=mesh,
        in_specs=(P("dp", None), P("dp", "vocab"), P("dp"), P("dp", None), P("dp"), P("dp")),
        out_specs=(P(), P("dp", "vocab"), P("dp", "vocab")),
        check_vma=False,
    )
```

time: 432 us -> 126 us (0.29)
  the two profiles are of different devices: /device:TPU:1 before, /device:TPU:5 now
where the time goes in v1:
time: 126 us
  Pallas kernels  116 us (92%)
  local copies, waits for them, and re-layouts  7 us (6%)
  between operations  2.48 us (2%)
    pallas_call x1, Pallas kernels, local(): pl.pallas_call(functools.partial(kernel, cfg), out_shape=(jax.ShapeDtypeS...  116 us
    unnamed x14, local copies, waits for them, and re-layouts  7 us

profile of v1, /device:TPU:5, one launch (start us, length us, event | category | flops | bytes accessed | tf_op | source)
XLA Modules:
  0.0 125.6 jit_solution(4966319576325299383)
XLA Ops:
  0.6 0.0 copy-start
  0.6 1.6 %copy-done = bf16[512,2048]{1,0:T(8,128)(2,1)S(1)} copy-done((bf16[512,2048]{1,0:T(8,128)(2,1)S(1)}, bf16[512,2048]{1,0:T(8,128)(2,1)}, u32[]{:S(2)}) %copy-start) | copy-done | bytes 2097176
  2.2 0.0 copy-start.1
  2.2 1.0 copy-done.1
  3.3 0.0 copy-start.2
  3.3 0.7 copy-done.2
  3.9 0.0 copy-start.3
  4.0 0.7 copy-done.3
  4.6 0.0 copy-start.4
  4.6 0.7 copy-done.4
  5.3 0.0 copy-start.5
  5.3 0.7 copy-done.5
  5.9 116.1 %shard_map.85 = (f32[1,1]{1,0:T(1,128)}, bf16[512,64]{1,0:T(8,128)(2,1)S(1)}, f32[128,2048]{1,0:T(8,128)S(1)}) custom-call(s32[2]{0:T(128)S(1)} %copy-done.4, s32[2]{0:T(128)S(1)} %copy-done.5, s32[2,256]{1,0:T(2,128)S(1)} %copy-done.2, s32[1,512]{1,0:T(1,128)S(1)} %bitcast.2, bf16[512,2048]{1,0:T(8,128)(2,1)S(1)} %copy-done, bf16[128,2048]{1,0:T(8,128)(2,1)S(1)} %copy-done.1), custom_call_target="tpu_custom_call" | custom-call | tf_op jit(solution)/shard_map/pallas_call | solution.py:590
  122.1 0.7 copy.9
  123.5 1.0 copy.13
Async XLA Ops:
  0.6 1.6 %copy-start = (bf16[512,2048]{1,0:T(8,128)(2,1)S(1)}, bf16[512,2048]{1,0:T(8,128)(2,1)}, u32[]{:S(2)}) copy-start(bf16[512,2048]{1,0:T(8,128)(2,1)} %states_ref.1) | copy-start | bytes 6291460
  2.2 1.0 copy-start.1
  3.3 0.7 copy-start.2
  3.9 0.7 copy-start.3
  4.6 0.7 copy-start.4
  5.3 0.7 copy-start.5

commit v2 on v0

v2 whole, which is shorter than its diff:
```python
import functools

import jax
import jax.numpy as jnp
from jax import lax
from jax.experimental import pallas as pl
from jax.experimental.pallas import tpu as pltpu
from jax.sharding import PartitionSpec as P

MESH = pl.DeviceIdType.MESH
F32 = jnp.float32
BF16 = jnp.bfloat16

CAP = 48
LIVE = 896
RATE_DEN = 1024
NX = 4
META = 16


def nn(a, b):
    return lax.dot_general(a, b, (((1,), (0,)), ((), ())), preferred_element_type=F32)


def nt(a, b):
    return lax.dot_general(a, b, (((1,), (1,)), ((), ())), preferred_element_type=F32)


def tn(a, b):
    return lax.dot_general(a, b, (((0,), (0,)), ((), ())), preferred_element_type=F32)


def iota(shape, dim):
    return lax.broadcasted_iota(jnp.int32, shape, dim)


def kernel(
    cfg,
    counts_hbm,
    rate_hbm,
    pos_hbm,
    tgt_hbm,
    states_hbm,
    w_hbm,
    loss_ref,
    gh_ref,
    gw_hbm,
    counts_ref,
    rate_ref,
    pos_ref,
    tgt_ref,
    w_ref,
    s_buf,
    pmt,
    blocks,
    wc,
    xg,
    e_buf,
    g_buf,
    xd,
    rank_buf,
    meta,
    qun,
    lse_y,
    lse_xz,
    loss_buf,
    gw_ref,
    ght,
    red,
    fin,
    u_buf,
    in_sem,
    a_sem,
    w_send,
    w_recv,
    wf_sem,
    core_send,
    core_recv,
    x_sem,
    zr_send,
    zr_recv,
    zu_send,
    zu_recv,
    xf_sem,
    e_send,
    e_recv,
    g_send,
    g_recv,
    ly_sem,
    lp_sem,
    r_send,
    r_recv,
    u_sem,
    out_sem,
):
    ny, nx, nz, vw, slots, tokens, seq, all_tokens = cfg
    ndp, nch = 2 * ny, nx * nz
    rg = LIVE // 4
    rp = rg // 2
    width = lse_y.shape[3]
    dg = 256 // nch

    dp = lax.axis_index("dp")
    vo = lax.axis_index("vocab")
    y, c = dp // 2, dp % 2
    x, z = vo // nz, vo % nz
    here = c * ny + y
    piece = z * nx + x
    m, h = piece // 2, piece % 2

    def rem(src, dst, send, recv, device):
        return pltpu.make_async_remote_copy(
            src_ref=src,
            dst_ref=dst,
            send_sem=send,
            recv_sem=recv,
            device_id=device,
            device_id_type=MESH,
        )

    def go(src, dst, send, recv, device):
        rem(src, dst, send, recv, device).start()

    def arrived(dst, recv):
        rem(dst, dst, recv, recv, (dp, vo)).wait_recv()

    def gone(src, send):
        rem(src, src, send, send, (dp, vo)).wait_send()

    def in_column(yy):
        return (2 * yy + c, vo)

    sibling = (2 * y + 1 - c, vo)
    peer_x = lambda xx: (dp, xx * nz + z)
    peer_z = lambda zz: (dp, x * nz + zz)

    states_slice = states_hbm.at[:, pl.ds(pl.multiple_of(m * 128, 128), 128)]
    loads = [
        pltpu.make_async_copy(src, dst, in_sem.at[i])
        for i, (src, dst) in enumerate(
            [
                (pos_hbm, pos_ref),
                (tgt_hbm, tgt_ref),
                (counts_hbm, counts_ref),
                (rate_hbm, rate_ref),
                (states_slice, s_buf),
                (w_hbm, w_ref.at[c]),
            ]
        )
    ]
    for load in loads:
        load.start()

    barrier = pltpu.get_barrier_semaphore()
    q = vo
    target_vo = 4 * y + q // (nch // 4)
    src_y, src_q0 = vo // 4, (nch // 4) * (vo % 4)
    to_self = target_vo == vo

    def signal(device):
        pl.semaphore_signal(barrier, inc=1, device_id=device, device_id_type=MESH)

    for k in range(1, ny):
        signal(in_column((y + k) % ny))
    signal(sibling)

    def signal_plane(k, carry):
        signal((dp, (vo + k) % nch))
        return carry

    lax.fori_loop(1, nch, signal_plane, 0)

    def signal_source(t, carry):
        source = (2 * src_y + t // (nch // 4), src_q0 + t % (nch // 4))

        @pl.when(jnp.logical_not((source[0] == dp) & (source[1] == vo)))
        def _():
            signal(source)

        return carry

    lax.fori_loop(0, nch // 2, signal_source, 0)

    loads[0].wait()
    lane = iota((8, 128), 1)
    pos0 = jnp.broadcast_to(pos_ref[0:1, 0:128], (8, 128))
    pos1 = jnp.broadcast_to(pos_ref[1:2, 0:128], (8, 128))
    pos1 = pltpu.roll(pos1, CAP, 1)
    tok = jnp.where(lane < CAP, pos0, jnp.where(lane < 2 * CAP, seq + pos1, -1))[0:1]
    pmt[...] = jnp.where(iota((tokens, 128), 0) == tok, 1.0, 0.0).astype(BF16)
    loads[1].wait()
    targets = tgt_ref[...]
    row16 = iota((META, tokens), 0)
    parts = jnp.where(
        row16 == 0,
        jnp.right_shift(targets, 8).astype(F32),
        jnp.where(row16 == 1, jnp.bitwise_and(targets, 255).astype(F32), 0.0),
    ).astype(BF16)
    label_rows = nn(parts, pmt[...])
    lane16 = iota((META, 128), 1)
    row16 = iota((META, 128), 0)

    def per_slot(first, second):
        return jnp.where(
            lane16 < CAP, first, jnp.where(lane16 < 2 * CAP, second, 0)
        ).astype(F32)

    loads[2].wait()
    loads[3].wait()
    r0, r1 = rate_ref[0], rate_ref[1]
    own_meta = jnp.where(
        row16 == 2, per_slot(jnp.right_shift(r0, 8), jnp.right_shift(r1, 8)), label_rows
    )
    own_meta = jnp.where(
        row16 == 3, per_slot(jnp.bitwise_and(r0, 255), jnp.bitwise_and(r1, 255)), own_meta
    )
    own_meta = jnp.where(row16 == 4, per_slot(counts_ref[0], counts_ref[1]), own_meta)
    loads[4].wait()
    chosen = tn(pmt[...], s_buf[...])
    blocks[c, y, 0:slots, :] = chosen[0:slots].astype(BF16)
    blocks[c, y, slots : slots + META, :] = own_meta.astype(BF16)

    n_to = (ny - 1) + 1 + (nch - 1)
    pl.semaphore_wait(barrier, n_to + ndp - jnp.where(to_self, 1, 0))

    for k in range(1, ny):
        go(blocks.at[c, y], blocks.at[c, y], a_sem.at[0], a_sem.at[1], in_column((y + k) % ny))
    loads[5].wait()

    def own_columns(o):
        return w_ref.at[c, :, pl.ds(pl.multiple_of(o * vw, vw), vw)]

    near = sorted(range(1, ny), key=lambda k: min(k, ny - k))
    for k in reversed(near):
        yy = (y + k) % ny
        go(own_columns(yy), wc.at[dp], w_send, w_recv.at[k], in_column(yy))
    wc[dp] = own_columns(y)[...]
    go(wc.at[dp], wc.at[dp], wf_sem.at[0], wf_sem.at[1], sibling)
    go(w_ref.at[c], w_ref.at[c], core_send.at[1], core_recv.at[1], sibling)
    arrived(blocks.at[c, 0 : ny - 1], a_sem.at[1])
    go(blocks.at[c], blocks.at[c], core_send.at[0], core_recv.at[0], sibling)
    arrived(blocks.at[1 - c], core_recv.at[0])

    all_meta = blocks[:, :, slots : slots + META, :].astype(F32).reshape(ndp, META, 128)
    count_rows = jnp.sum(
        jnp.where(iota((ndp, META, 128), 1) == 4, all_meta, 0.0), axis=1
    )
    first, second = count_rows[:, 0:1], count_rows[:, CAP : CAP + 1]
    in_all = jnp.broadcast_to(first + second, (ndp, 128)).astype(BF16)

    def order(v):
        return 2 * (v % ny) + v // ny

    earlier = jnp.where(
        order(iota((ndp, ndp), 1)) < order(iota((ndp, ndp), 0)), 1.0, 0.0
    ).astype(BF16)
    offset = nn(earlier, in_all)
    lanes = iota((ndp, 128), 1).astype(F32)
    in_first = lanes < CAP
    place = jnp.where(in_first, lanes, lanes - CAP + first)
    bound = jnp.where(in_first, first, second)
    local_place = jnp.where(in_first, lanes, lanes - CAP)
    live = (local_place < bound) & (lanes < 2 * CAP)
    rank_buf[...] = jnp.where(live, offset + place, -1.0)

    def one_hot(start, rows, a):
        names = iota((rows, 128), 0) + start
        return jnp.where(names.astype(F32) == rank_buf[a : a + 1, :], 1.0, 0.0).astype(BF16)

    for t in range(2):
        acc = jnp.zeros((rp, 128), F32)
        for a in range(ndp):
            pick = one_hot((2 * c + t) * rg + h * rp, rp, a)
            acc += nn(pick[:, 0:slots], blocks[a // ny, a % ny, 0:slots, :])
        xg[t, piece] = acc.astype(BF16)
        own = xg.at[t, piece]
        if t == 0:
            for k in range(1, nx):
                go(own, own, x_sem.at[0], x_sem.at[1], peer_x((x + k) % nx))
        else:
            for k in sorted(range(1, nz), key=lambda k: min(k, nz - k)):
                go(own, own, zu_send, zu_recv.at[k], peer_z((z + k) % nz))
            for k in range(1, nx):
                go(own, own, xf_sem.at[0], xf_sem.at[1], peer_x((x + k) % nx))

    def metas(t):
        total = jnp.zeros((rg, META), F32)
        for a in range(ndp):
            pick = one_hot((2 * c + t) * rg, rg, a)
            qun[t, :, a * 128 : (a + 1) * 128] = pick
            total += nt(pick, blocks[a // ny, a % ny, slots : slots + META, :])
        meta[t] = total

    def ring(n, me, block, subs, send, recv, device):
        last = n // 2 - 1

        def moves(step):
            for sub in range(subs):
                for way in (0, 1):
                    if step < last or (sub < subs // 2) == (way == 0):
                        yield way, sub

        def start(step):
            for way, sub in moves(step):
                start_one(step, way, sub)

        def start_one(step, way, sub):
            origin = (me + n - step) % n if way == 0 else (me + step) % n
            to = (me + 1) % n if way == 0 else (me + n - 1) % n
            ref = block(origin, sub)
            go(ref, ref, send, recv.at[way, step, sub], device(to))

        def advance(step, then=None):
            following = set(moves(step + 1)) if step < last else set()
            for way, sub in moves(step):
                origin = (me + n - 1 - step) % n if way == 0 else (me + 1 + step) % n
                ref = block(origin, sub)
                arrived(ref, recv.at[way, step, sub])
                if (way, sub) in following:
                    start_one(step + 1, way, sub)
                if then is not None:
                    then((n - 1 - step) if way == 0 else 1 + step, sub)

        return last, start, advance

    half_x = nx // 2
    x_last, x_start, x_advance = ring(
        nz,
        z,
        lambda o, sub: xg.at[0, pl.ds(o * nx + sub * half_x, half_x)],
        2,
        zr_send,
        zr_recv,
        peer_z,
    )

    def pass_on(k):
        ref = xg.at[1, ((z + nz - k) % nz) * nx + x]
        arrived(ref, zu_recv.at[k])
        for i in range(1, nx):
            go(ref, ref, xf_sem.at[0], xf_sem.at[1], peer_x((x + i) % nx))

    def w_arrive(k):
        ref = wc.at[2 * ((y + ny - k) % ny) + c]
        arrived(ref, w_recv.at[k])
        go(ref, ref, wf_sem.at[0], wf_sem.at[1], sibling)

    z_near = sorted(range(1, nz), key=lambda k: min(k, nz - k))
    w_near = list(near)
    arrived(xg.at[0, 0 : nx - 1], x_sem.at[1])
    x_start(0)
    for k in z_near[:2]:
        pass_on(k)
    z_near = z_near[2:]
    metas(0)
    for step in range(x_last + 1):
        x_advance(step)
        take = 2 if step < x_last else len(z_near)
        for k in z_near[:take]:
            pass_on(k)
        z_near = z_near[take:]
        if step == 0:
            metas(1)
        take = 2 if step < x_last else len(w_near)
        for k in w_near[:take]:
            w_arrive(k)
        w_near = w_near[take:]
    arrived(wc.at[0:ny], wf_sem.at[1])

    def label_of(t):
        rows = meta[t]
        return (rows[:, 0:1] * 256.0 + rows[:, 1:2]).astype(jnp.int32)

    def weight_of(t):
        rows = meta[t]
        return RATE_DEN / (rows[:, 2:3] * 256.0 + rows[:, 3:4])

    e_rings = [
        ring(
            ny,
            y,
            lambda o, sub, t=t: e_buf.at[t, o, sub],
            2,
            e_send.at[t],
            e_recv.at[t],
            in_column,
        )
        for t in range(2)
    ]
    e_last = e_rings[0][0]

    def softmax_part(t):
        logits = jnp.zeros((rg, vw), F32)
        for mm in range(0, ndp, 2):
            rows = [xg[t, 2 * (mm + i) : 2 * (mm + i) + 2].reshape(rg, 128) for i in range(2)]
            logits += nn(
                jnp.concatenate(rows, axis=1), wc[mm : mm + 2].reshape(256, vw)
            )
        high = jnp.max(logits, axis=1, keepdims=True)
        powers = jnp.exp(logits - high)
        sums = jnp.sum(powers, axis=1, keepdims=True)
        lse = high + jnp.log(sums)
        own_part = powers * (1.0 / sums)
        for sub in range(2):
            e_buf[t, y, sub] = own_part[sub * rp : (sub + 1) * rp].astype(BF16)
        hit = iota((rg, vw), 1) == label_of(t) - (vo * (vw * ny) + y * vw)
        of_targets = jnp.sum(
            jnp.sum(jnp.where(hit, logits * weight_of(t), 0.0), axis=1, keepdims=True),
            axis=0,
            keepdims=True,
        )
        lse_row = jnp.transpose(jnp.broadcast_to(lse, (rg, 128)))[0:1]
        lse_y[y, t, :, 0:rg] = lse_row
        lse_y[y, t, :, rg:width] = jnp.broadcast_to(of_targets, (1, width - rg))
        go(
            xg.at[t, pl.ds(2 * (dp + 1 - 2 * c), 2)],
            xd.at[c, t],
            core_send.at[2 + t],
            core_recv.at[2 + t],
            sibling,
        )
        xd[c, t] = xg[t, pl.ds(2 * dp, 2)]

    in_rows = iota((1, width), 1) < rg

    def combine(rows):
        top = functools.reduce(jnp.maximum, rows)
        exps = functools.reduce(jnp.add, [jnp.exp(r - top) for r in rows])
        plain = functools.reduce(jnp.add, rows)
        return jnp.where(in_rows, top + jnp.log(exps), plain)

    def send_stats():
        for k in range(1, ny):
            go(lse_y.at[y], lse_y.at[y], ly_sem.at[0], ly_sem.at[1], in_column((y + k) % ny))

    def column_stats():
        arrived(lse_y.at[0 : ny - 1], ly_sem.at[1])
        for t in range(2):
            lse_xz[vo, t] = combine([lse_y[i, t] for i in range(ny)])

        def send(k, carry):
            go(lse_xz.at[vo], lse_xz.at[vo], lp_sem.at[0], lp_sem.at[1], (dp, (vo + k) % nch))
            return carry

        lax.fori_loop(1, nch, send, 0)

    features, scales, labels, weights = {}, {}, {}, {}

    def plane_stats():
        arrived(lse_xz.at[0 : nch - 1], lp_sem.at[1])
        loss = jnp.zeros((1, 1), F32)
        for t in range(2):
            log_total = combine([lse_xz[i, t] for i in range(nch)])
            rows = [lse_y[(y + k) % ny, t] for k in range(ny)] + [log_total]
            rows += [jnp.zeros_like(log_total)] * (-len(rows) % 8)
            cols = jnp.transpose(jnp.concatenate(rows, axis=0))[0:rg]
            labels[t], weights[t] = label_of(t), weight_of(t)
            total_col = cols[:, ny : ny + 1]
            scales[t] = weights[t] * jnp.exp(cols - total_col)
            loss += jnp.sum(weights[t] * total_col, axis=0, keepdims=True)
            loss -= log_total[:, rg : rg + 1]
        loss_buf[c] = jnp.broadcast_to(loss, loss_buf.shape[1:])
        go(loss_buf.at[c], loss_buf.at[c], core_send.at[4], core_recv.at[4], sibling)
        arrived(w_ref.at[1 - c], core_recv.at[1])
        for t in range(2):
            features[t] = jnp.transpose(xd[c, t].reshape(rg, 128))

    def own(t, offset):
        o = (y + offset) % ny
        columns = pl.ds(pl.multiple_of(o * vw, vw), vw)
        part = e_buf[t, o].reshape(rg, vw).astype(F32)
        hit = iota((rg, vw), 1) == labels[t] - (vo * (vw * ny) + o * vw)
        scaled = part * scales[t][:, offset : offset + 1]
        g_logits = jnp.where(hit, scaled - weights[t], scaled).astype(BF16)
        g_buf[c, t, o] = g_logits
        go(g_buf.at[c, t, o], g_buf.at[c, t, o], g_send, g_recv.at[t, offset], sibling)
        term = nt(w_ref[:, :, columns].reshape(256, vw), g_logits)
        if offset == 0:
            ght[t] = term
        else:
            ght[t] += term
        grad = nn(features[t], g_logits)
        if t == 0:
            gw_ref[:, columns] = grad
        else:
            gw_ref[:, columns] += grad

    def others():
        for t in range(2):
            arrived(xd.at[1 - c, t], core_recv.at[2 + t])
        turned = [jnp.transpose(xd[1 - c, t].reshape(rg, 128)) for t in range(2)]
        for offset in range(ny):
            o = (y + offset) % ny
            columns = pl.ds(pl.multiple_of(o * vw, vw), vw)
            grad = gw_ref[:, columns]
            for t in range(2):
                arrived(g_buf.at[1 - c, t, o], g_recv.at[t, offset])
                grad += nn(turned[t], g_buf[1 - c, t, o])
            gw_ref[:, columns] = grad

    def piece_of(t, qq):
        return ght.at[t, pl.ds(pl.multiple_of(qq * dg, dg), dg), :]

    def send_pieces(t):
        def send(k, carry):
            to = (vo + k) % nch
            go(piece_of(t, to), red.at[t, vo], r_send, r_recv.at[t], (dp, to))
            return carry

        lax.fori_loop(1, nch, send, 0)
        red[t, vo] = piece_of(t, vo)[...]

    def add_pieces(t):
        arrived(red.at[t, 0 : nch - 1], r_recv.at[t])
        return nn(jnp.sum(red[t], axis=0).astype(BF16), qun[t])

    softmax_part(0)
    e_rings[0][1](0)
    arrived(xg.at[1, 0 : (nx - 1) * nz], xf_sem.at[1])
    softmax_part(1)
    send_stats()
    e_rings[1][1](0)
    arrival = [sorted({ny - 1 - s, 1 + s}) for s in range(e_last + 1)]
    ready = {0: [0], 1: [0]}

    def spread(t, step):
        e_rings[t][2](step)
        ready[t] += arrival[step]

    def work(t, count):
        for _ in range(min(count, len(ready[t]))):
            offset = ready[t].pop(0)
            own(t, offset)
            if offset == ny // 2:
                send_pieces(t)

    spread(0, 0)
    column_stats()
    spread(1, 0)
    if e_last > 0:
        spread(0, 1)
    plane_stats()
    for step in range(1, e_last + 1):
        spread(1, step)
        work(0, 4)
        if step < e_last:
            spread(0, step + 1)
            work(0, 2)
            work(1, 1)
    work(0, ny)
    work(1, ny)
    others()
    gw_copy = pltpu.make_async_copy(gw_ref, gw_hbm, out_sem)
    gw_copy.start()
    arrived(loss_buf.at[1 - c], core_recv.at[4])
    loss_ref[...] = (loss_buf[0, :, 0:1] + loss_buf[1, :, 0:1]) * (1.0 / all_tokens)
    in_slots = add_pieces(0)
    in_slots += add_pieces(1)
    for a in range(ndp):
        fin[a] = in_slots[:, a * 128 : (a + 1) * 128]
    slot = c * (nch // 4) + q % (nch // 4)

    def send_final(a, carry):
        @pl.when(jnp.logical_not(to_self & (a == here)))
        def _():
            to = (2 * (a % ny) + a // ny, target_vo)
            go(fin.at[a], u_buf.at[slot], u_sem.at[0], u_sem.at[1], to)

        return carry

    lax.fori_loop(0, ndp, send_final, 0)

    @pl.when(to_self)
    def _():
        u_buf[slot] = fin[here]

    gone(blocks.at[c, 0 : ny - 1], a_sem.at[0])
    gone(wc.at[0 : ny - 1], w_send)
    gone(wc.at[0:ny], wf_sem.at[0])
    gone(blocks.at[c], core_send.at[0])
    gone(w_ref.at[c], core_send.at[1])
    for t in range(2):
        gone(xd.at[c, t], core_send.at[2 + t])
        gone(e_buf.at[t, 0 : ny - 1], e_send.at[t])
    gone(loss_buf.at[c], core_send.at[4])
    gone(xg.at[0, 0 : nx - 1], x_sem.at[0])
    gone(xg.at[0, 0 : (nz - 1) * nx], zr_send)
    gone(xg.at[1, 0 : nz - 1], zu_send)
    gone(xg.at[1, 0 : (nx - 1) * nz], xf_sem.at[0])
    gone(lse_y.at[0 : ny - 1], ly_sem.at[0])
    gone(lse_xz.at[0 : nch - 1], lp_sem.at[0])
    gone(g_buf.at[c], g_send)
    gone(red.at[:, 0 : nch - 1], r_send)
    gw_copy.wait()

    @pl.when(to_self)
    def _():
        arrived(u_buf.at[0 : nch // 2 - 1], u_sem.at[1])
        gone(fin.at[0 : ndp - 1], u_sem.at[0])

    @pl.when(jnp.logical_not(to_self))
    def _():
        arrived(u_buf, u_sem.at[1])
        gone(fin, u_sem.at[0])

    half = nch // 4
    pieces = [u_buf[t] + u_buf[half + t] for t in range(half)]
    columns = jnp.concatenate(pieces, axis=0).astype(BF16)
    gh_ref[...] = nt(columns, pmt[...]).astype(BF16)


def copies(loss, gh, gw, loss_out, gh_out, gw_out, loss_buf, gh_buf, gw_buf, sems):
    rows = gw.shape[0] // 4
    moves = [(loss, loss_buf, loss_out), (gh, gh_buf, gh_out)]
    moves += [tuple(r.at[pl.ds(k * rows, rows)] for r in (gw, gw_buf, gw_out)) for k in range(4)]
    into = [pltpu.make_async_copy(a, b, sems.at[0, k]) for k, (a, b, _) in enumerate(moves)]
    out = [pltpu.make_async_copy(b, d, sems.at[1, k]) for k, (_, b, d) in enumerate(moves)]
    for move in into:
        move.start()
    for first, then in zip(into, out):
        first.wait()
        then.start()
    for move in out:
        move.wait()


def local(states, head_weight, targets, positions, counts, rate_num):
    ndp = lax.axis_size("dp")
    nch = lax.axis_size("vocab")
    ny, nx, nz = ndp // 2, NX, nch // NX
    tokens, d = states.shape
    vw = head_weight.shape[1] // ny
    seqs, seq = positions.shape
    slots = seqs * CAP
    rg = LIVE // 4
    width = -(-(rg + 1) // 128) * 128
    dg = 256 // nch
    cfg = (ny, nx, nz, vw, slots, tokens, seq, ndp * tokens)
    dma = pltpu.SemaphoreType.DMA
    scratch = [
        pltpu.SMEM(counts.shape, jnp.int32),
        pltpu.SMEM(rate_num.shape, jnp.int32),
        pltpu.VMEM(positions.shape, jnp.int32),
        pltpu.VMEM((1, tokens), jnp.int32),
        pltpu.VMEM((2,) + head_weight.shape, BF16),
        pltpu.VMEM((tokens, 128), BF16),
        pltpu.VMEM((tokens, 128), BF16),
        pltpu.VMEM((2, ny, slots + META, 128), BF16),
        pltpu.VMEM((ndp, 128, vw), BF16),
        pltpu.VMEM((2, nch, rg // 2, 128), BF16),
        pltpu.VMEM((2, ny, 2, rg // 2, vw), BF16),
        pltpu.VMEM((2, 2, ny, rg, vw), BF16),
        pltpu.VMEM((2, 2, 2, rg // 2, 128), BF16),
        pltpu.VMEM((ndp, 128), F32),
        pltpu.VMEM((2, rg, META), F32),
        pltpu.VMEM((2, rg, ndp * 128), BF16),
        pltpu.VMEM((ny, 2, 1, width), F32),
        pltpu.VMEM((nch, 2, 1, width), F32),
        pltpu.VMEM((2, 1, 128), F32),
        pltpu.VMEM(head_weight.shape, F32),
        pltpu.VMEM((2, 256, rg), F32),
        pltpu.VMEM((2, nch, dg, rg), F32),
        pltpu.VMEM((ndp, dg, 128), F32),
        pltpu.VMEM((nch // 2, dg, 128), F32),
        dma((6,)),
        dma((2,)),
        dma,
        dma((ny,)),
        dma((2,)),
        dma((5,)),
        dma((5,)),
        dma((2,)),
        dma,
        dma((2, nz // 2, 2)),
        dma,
        dma((nz,)),
        dma((2,)),
        dma((2,)),
        dma((2, 2, ny // 2, 2)),
        dma,
        dma((2, ny)),
        dma((2,)),
        dma((2,)),
        dma,
        dma((2,)),
        dma((2,)),
        dma,
    ]
    vmem = pl.BlockSpec(memory_space=pltpu.VMEM)
    hbm = pl.BlockSpec(memory_space=pltpu.HBM)
    out_shape = (
        jax.ShapeDtypeStruct((1, 1), F32),
        jax.ShapeDtypeStruct((d // nch, tokens), BF16),
        jax.ShapeDtypeStruct(head_weight.shape, F32),
    )
    results = pl.pallas_call(
        functools.partial(kernel, cfg),
        out_shape=out_shape,
        in_specs=[hbm] * 6,
        out_specs=(vmem, vmem, hbm),
        scratch_shapes=scratch,
        compiler_params=pltpu.CompilerParams(
            collective_id=0, has_side_effects=True, vmem_limit_bytes=63 * 1024 * 1024
        ),
    )(counts, rate_num, positions, targets.reshape(1, tokens), states, head_weight)
    loss, grad_hidden, grad_weight = pl.pallas_call(
        copies,
        out_shape=out_shape,
        in_specs=[hbm] * 3,
        out_specs=(hbm,) * 3,
        scratch_shapes=[pltpu.VMEM(o.shape, o.dtype) for o in out_shape] + [dma((2, 6))],
        compiler_params=pltpu.CompilerParams(vmem_limit_bytes=63 * 1024 * 1024),
    )(*results)
    return loss[0, 0], grad_hidden.T, grad_weight


def solution(mesh):
    return jax.shard_map(
        local,
        mesh=mesh,
        in_specs=(P("dp", None), P("dp", "vocab"), P("dp"), P("dp", None), P("dp"), P("dp")),
        out_specs=(P(), P("dp", "vocab"), P("dp", "vocab")),
        check_vma=False,
    )
```

time: 432 us -> 100 us (0.23)
  the two profiles are of different devices: /device:TPU:1 before, /device:TPU:5 now
where the time goes in v2:
time: 100 us
  Pallas kernels  99.3 us (99%)
    pallas_call x1, Pallas kernels, local(): pl.pallas_call(functools.partial(kernel, cfg), out_shape=out_shape, in_sp...  96.7 us
    pallas_call x1, Pallas kernels, local(): pl.pallas_call(copies, out_shape=out_shape, in_specs=[hbm] * 3, out_specs...  2.68 us

profile of v2, /device:TPU:5, one launch (start us, length us, event | category | flops | bytes accessed | tf_op | source)
XLA Modules:
  0.0 100.0 jit_solution(3732104045968711733)
XLA Ops:
  0.6 96.7 %shard_map.85 = (f32[1,1]{1,0:T(1,128)}, bf16[64,512]{1,0:T(8,128)(2,1)}, f32[128,2048]{1,0:T(8,128)}) custom-call(s32[2]{0:T(128)} %counts_hbm.1, s32[2]{0:T(128)} %rate_hbm.1, s32[2,256]{1,0:T(2,128)} %pos_hbm.1, s32[1,512]{1,0:T(1,128)} %bitcast.3, bf16[512,2048]{1,0:T(8,128)(2,1)} %states_hbm.1, bf16[128,2048]{1,0:T(8,128)(2,1)} %w_hbm.1), custom_call_target="tpu_custom_call" | custom-call | tf_op jit(solution)/shard_map/pallas_call | solution.py:696
  97.3 2.7 %shard_map.86 = (f32[1,1]{1,0:T(1,128)}, bf16[64,512]{1,0:T(8,128)(2,1)}, f32[128,2048]{1,0:T(8,128)}) custom-call(f32[1,1]{1,0:T(1,128)} %get-tuple-element.9.loss, bf16[64,512]{1,0:T(8,128)(2,1)} %get-tuple-element.10.gh, f32[128,2048]{1,0:T(8,128)} %get-tuple-element.11.gw), custom_call_target="tpu_custom_call" | custom-call | tf_op jit(solution)/shard_map/pallas_call | solution.py:706

commit v3 on v2

--- a/solution.py
+++ b/solution.py
@@ -54,19 +54,29 @@
     pmt,
     blocks,
     wc,
-    xg,
-    e_buf,
-    g_buf,
-    xd,
+    xg_0,
+    xg_1,
+    e_buf_0,
+    e_buf_1,
+    g_buf_0,
+    g_buf_1,
+    xd_0,
+    xd_1,
     rank_buf,
-    meta,
-    qun,
-    lse_y,
-    lse_xz,
+    meta_0,
+    meta_1,
+    qun_0,
+    qun_1,
+    lse_y_0,
+    lse_y_1,
+    lse_xz_0,
+    lse_xz_1,
     loss_buf,
     gw_ref,
-    ght,
-    red,
+    ght_0,
+    ght_1,
+    red_0,
+    red_1,
     fin,
     u_buf,
     in_sem,
@@ -86,18 +96,23 @@
     e_recv,
     g_send,
     g_recv,
-    ly_sem,
-    lp_sem,
+    ly_send,
+    ly_recv,
+    lp_send,
+    lp_recv,
     r_send,
     r_recv,
     u_sem,
     out_sem,
 ):
-    ny, nx, nz, vw, slots, tokens, seq, all_tokens = cfg
+    ny, nx, nz, vw, slots, tokens, seq, all_tokens, piece_rows = cfg
     ndp, nch = 2 * ny, nx * nz
-    rg = LIVE // 4
-    rp = rg // 2
-    width = lse_y.shape[3]
+    xg, e_buf, g_buf, xd = (xg_0, xg_1), (e_buf_0, e_buf_1), (g_buf_0, g_buf_1), (xd_0, xd_1)
+    meta, qun, ght, red = (meta_0, meta_1), (qun_0, qun_1), (ght_0, ght_1), (red_0, red_1)
+    lse_y, lse_xz = (lse_y_0, lse_y_1), (lse_xz_0, lse_xz_1)
+    rps = piece_rows
+    rgs = [2 * r for r in rps]
+    widths = [r.shape[2] for r in lse_y]
     dg = 256 // nch
 
     dp = lax.axis_index("dp")
@@ -230,16 +245,15 @@
     def own_columns(o):
         return w_ref.at[c, :, pl.ds(pl.multiple_of(o * vw, vw), vw)]
 
+    arrived(blocks.at[c, 0 : ny - 1], a_sem.at[1])
+    go(blocks.at[c], blocks.at[c], core_send.at[0], core_recv.at[0], sibling)
     near = sorted(range(1, ny), key=lambda k: min(k, ny - k))
     for k in reversed(near):
         yy = (y + k) % ny
         go(own_columns(yy), wc.at[dp], w_send, w_recv.at[k], in_column(yy))
     wc[dp] = own_columns(y)[...]
+    arrived(blocks.at[1 - c], core_recv.at[0])
     go(wc.at[dp], wc.at[dp], wf_sem.at[0], wf_sem.at[1], sibling)
-    go(w_ref.at[c], w_ref.at[c], core_send.at[1], core_recv.at[1], sibling)
-    arrived(blocks.at[c, 0 : ny - 1], a_sem.at[1])
-    go(blocks.at[c], blocks.at[c], core_send.at[0], core_recv.at[0], sibling)
-    arrived(blocks.at[1 - c], core_recv.at[0])
 
     all_meta = blocks[:, :, slots : slots + META, :].astype(F32).reshape(ndp, META, 128)
     count_rows = jnp.sum(
@@ -263,33 +277,30 @@
     live = (local_place < bound) & (lanes < 2 * CAP)
     rank_buf[...] = jnp.where(live, offset + place, -1.0)
 
+    def first_row(t):
+        return c * (LIVE // 2) + (rgs[0] if t else 0)
+
     def one_hot(start, rows, a):
         names = iota((rows, 128), 0) + start
         return jnp.where(names.astype(F32) == rank_buf[a : a + 1, :], 1.0, 0.0).astype(BF16)
 
-    for t in range(2):
+    def own_piece(t):
+        rp = rps[t]
         acc = jnp.zeros((rp, 128), F32)
         for a in range(ndp):
-            pick = one_hot((2 * c + t) * rg + h * rp, rp, a)
+            pick = one_hot(first_row(t) + h * rp, rp, a)
             acc += nn(pick[:, 0:slots], blocks[a // ny, a % ny, 0:slots, :])
-        xg[t, piece] = acc.astype(BF16)
-        own = xg.at[t, piece]
-        if t == 0:
-            for k in range(1, nx):
-                go(own, own, x_sem.at[0], x_sem.at[1], peer_x((x + k) % nx))
-        else:
-            for k in sorted(range(1, nz), key=lambda k: min(k, nz - k)):
-                go(own, own, zu_send, zu_recv.at[k], peer_z((z + k) % nz))
-            for k in range(1, nx):
-                go(own, own, xf_sem.at[0], xf_sem.at[1], peer_x((x + k) % nx))
+        xg[t][piece] = acc.astype(BF16)
+        return xg[t].at[piece]
 
     def metas(t):
+        rg = rgs[t]
         total = jnp.zeros((rg, META), F32)
         for a in range(ndp):
-            pick = one_hot((2 * c + t) * rg, rg, a)
-            qun[t, :, a * 128 : (a + 1) * 128] = pick
+            pick = one_hot(first_row(t), rg, a)
+            qun[t][:, a * 128 : (a + 1) * 128] = pick
             total += nt(pick, blocks[a // ny, a % ny, slots : slots + META, :])
-        meta[t] = total
+        meta[t][...] = total
 
     def ring(n, me, block, subs, send, recv, device):
         last = n // 2 - 1
@@ -327,7 +338,7 @@
     x_last, x_start, x_advance = ring(
         nz,
         z,
-        lambda o, sub: xg.at[0, pl.ds(o * nx + sub * half_x, half_x)],
+        lambda o, sub: xg[1].at[pl.ds(o * nx + sub * half_x, half_x)],
         2,
         zr_send,
         zr_recv,
@@ -335,8 +346,9 @@
     )
 
     def pass_on(k):
-        ref = xg.at[1, ((z + nz - k) % nz) * nx + x]
-        arrived(ref, zu_recv.at[k])
+        ref = xg[0].at[((z + nz - k) % nz) * nx + x]
+        if k > 0:
+            arrived(ref, zu_recv.at[k])
         for i in range(1, nx):
             go(ref, ref, xf_sem.at[0], xf_sem.at[1], peer_x((x + i) % nx))
 
@@ -347,39 +359,52 @@
 
     z_near = sorted(range(1, nz), key=lambda k: min(k, nz - k))
     w_near = list(near)
-    arrived(xg.at[0, 0 : nx - 1], x_sem.at[1])
+
+    def take(todo, count, do):
+        for _ in range(min(count, len(todo))):
+            do(todo.pop(0))
+
+    def rows_come(step):
+        if step <= x_last:
+            x_advance(step)
+
+    mine = own_piece(0)
+    for k in z_near:
+        go(mine, mine, zu_send, zu_recv.at[k], peer_z((z + k) % nz))
+    pass_on(0)
+    mine = own_piece(1)
+    for k in range(1, nx):
+        go(mine, mine, x_sem.at[0], x_sem.at[1], peer_x((x + k) % nx))
+    arrived(xg[1].at[0 : nx - 1], x_sem.at[1])
     x_start(0)
-    for k in z_near[:2]:
-        pass_on(k)
-    z_near = z_near[2:]
+    take(z_near, 4, pass_on)
+    metas(1)
+    rows_come(0)
+    take(z_near, 2, pass_on)
+    take(w_near, 2, w_arrive)
+    rows_come(1)
+    take(z_near, nz, pass_on)
     metas(0)
-    for step in range(x_last + 1):
-        x_advance(step)
-        take = 2 if step < x_last else len(z_near)
-        for k in z_near[:take]:
-            pass_on(k)
-        z_near = z_near[take:]
-        if step == 0:
-            metas(1)
-        take = 2 if step < x_last else len(w_near)
-        for k in w_near[:take]:
-            w_arrive(k)
-        w_near = w_near[take:]
+    take(w_near, 2, w_arrive)
+    rows_come(2)
+    take(w_near, ny, w_arrive)
+    go(w_ref.at[c], w_ref.at[c], core_send.at[1], core_recv.at[1], sibling)
+    arrived(xg[0].at[0 : (nx - 1) * nz], xf_sem.at[1])
     arrived(wc.at[0:ny], wf_sem.at[1])
 
     def label_of(t):
-        rows = meta[t]
+        rows = meta[t][...]
         return (rows[:, 0:1] * 256.0 + rows[:, 1:2]).astype(jnp.int32)
 
     def weight_of(t):
-        rows = meta[t]
+        rows = meta[t][...]
         return RATE_DEN / (rows[:, 2:3] * 256.0 + rows[:, 3:4])
 
     e_rings = [
         ring(
             ny,
             y,
-            lambda o, sub, t=t: e_buf.at[t, o, sub],
+            lambda o, sub, t=t: e_buf[t].at[o, sub],
             2,
             e_send.at[t],
             e_recv.at[t],
@@ -390,9 +415,10 @@
     e_last = e_rings[0][0]
 
     def softmax_part(t):
+        rg, rp, width = rgs[t], rps[t], widths[t]
         logits = jnp.zeros((rg, vw), F32)
         for mm in range(0, ndp, 2):
-            rows = [xg[t, 2 * (mm + i) : 2 * (mm + i) + 2].reshape(rg, 128) for i in range(2)]
+            rows = [xg[t][2 * (mm + i) : 2 * (mm + i) + 2].reshape(rg, 128) for i in range(2)]
             logits += nn(
                 jnp.concatenate(rows, axis=1), wc[mm : mm + 2].reshape(256, vw)
             )
@@ -402,7 +428,7 @@
         lse = high + jnp.log(sums)
         own_part = powers * (1.0 / sums)
         for sub in range(2):
-            e_buf[t, y, sub] = own_part[sub * rp : (sub + 1) * rp].astype(BF16)
+            e_buf[t][y, sub] = own_part[sub * rp : (sub + 1) * rp].astype(BF16)
         hit = iota((rg, vw), 1) == label_of(t) - (vo * (vw * ny) + y * vw)
         of_targets = jnp.sum(
             jnp.sum(jnp.where(hit, logits * weight_of(t), 0.0), axis=1, keepdims=True),
@@ -410,75 +436,74 @@
             keepdims=True,
         )
         lse_row = jnp.transpose(jnp.broadcast_to(lse, (rg, 128)))[0:1]
-        lse_y[y, t, :, 0:rg] = lse_row
-        lse_y[y, t, :, rg:width] = jnp.broadcast_to(of_targets, (1, width - rg))
+        lse_y[t][y, :, 0:rg] = lse_row
+        lse_y[t][y, :, rg:width] = jnp.broadcast_to(of_targets, (1, width - rg))
+        for k in range(1, ny):
+            ref = lse_y[t].at[y]
+            go(ref, ref, ly_send.at[t], ly_recv.at[t], in_column((y + k) % ny))
+        e_rings[t][1](0)
         go(
-            xg.at[t, pl.ds(2 * (dp + 1 - 2 * c), 2)],
-            xd.at[c, t],
+            xg[t].at[pl.ds(2 * (dp + 1 - 2 * c), 2)],
+            xd[t].at[c],
             core_send.at[2 + t],
             core_recv.at[2 + t],
             sibling,
         )
-        xd[c, t] = xg[t, pl.ds(2 * dp, 2)]
-
-    in_rows = iota((1, width), 1) < rg
-
-    def combine(rows):
+        xd[t][c] = xg[t][pl.ds(2 * dp, 2)]
+
+    def combine(t, rows):
         top = functools.reduce(jnp.maximum, rows)
         exps = functools.reduce(jnp.add, [jnp.exp(r - top) for r in rows])
         plain = functools.reduce(jnp.add, rows)
+        in_rows = iota((1, widths[t]), 1) < rgs[t]
         return jnp.where(in_rows, top + jnp.log(exps), plain)
 
-    def send_stats():
-        for k in range(1, ny):
-            go(lse_y.at[y], lse_y.at[y], ly_sem.at[0], ly_sem.at[1], in_column((y + k) % ny))
-
-    def column_stats():
-        arrived(lse_y.at[0 : ny - 1], ly_sem.at[1])
-        for t in range(2):
-            lse_xz[vo, t] = combine([lse_y[i, t] for i in range(ny)])
+    def column_stats(t):
+        arrived(lse_y[t].at[0 : ny - 1], ly_recv.at[t])
+        lse_xz[t][vo] = combine(t, [lse_y[t][i] for i in range(ny)])
 
         def send(k, carry):
-            go(lse_xz.at[vo], lse_xz.at[vo], lp_sem.at[0], lp_sem.at[1], (dp, (vo + k) % nch))
+            ref = lse_xz[t].at[vo]
+            go(ref, ref, lp_send.at[t], lp_recv.at[t], (dp, (vo + k) % nch))
             return carry
 
         lax.fori_loop(1, nch, send, 0)
 
-    features, scales, labels, weights = {}, {}, {}, {}
-
-    def plane_stats():
-        arrived(lse_xz.at[0 : nch - 1], lp_sem.at[1])
-        loss = jnp.zeros((1, 1), F32)
-        for t in range(2):
-            log_total = combine([lse_xz[i, t] for i in range(nch)])
-            rows = [lse_y[(y + k) % ny, t] for k in range(ny)] + [log_total]
-            rows += [jnp.zeros_like(log_total)] * (-len(rows) % 8)
-            cols = jnp.transpose(jnp.concatenate(rows, axis=0))[0:rg]
-            labels[t], weights[t] = label_of(t), weight_of(t)
-            total_col = cols[:, ny : ny + 1]
-            scales[t] = weights[t] * jnp.exp(cols - total_col)
-            loss += jnp.sum(weights[t] * total_col, axis=0, keepdims=True)
-            loss -= log_total[:, rg : rg + 1]
-        loss_buf[c] = jnp.broadcast_to(loss, loss_buf.shape[1:])
-        go(loss_buf.at[c], loss_buf.at[c], core_send.at[4], core_recv.at[4], sibling)
-        arrived(w_ref.at[1 - c], core_recv.at[1])
-        for t in range(2):
-            features[t] = jnp.transpose(xd[c, t].reshape(rg, 128))
+    features, scales, labels, weights, losses = {}, {}, {}, {}, {}
+
+    def plane_stats(t):
+        rg = rgs[t]
+        arrived(lse_xz[t].at[0 : nch - 1], lp_recv.at[t])
+        log_total = combine(t, [lse_xz[t][i] for i in range(nch)])
+        rows = [lse_y[t][(y + k) % ny] for k in range(ny)] + [log_total]
+        rows += [jnp.zeros_like(log_total)] * (-len(rows) % 8)
+        cols = jnp.transpose(jnp.concatenate(rows, axis=0))[0:rg]
+        labels[t], weights[t] = label_of(t), weight_of(t)
+        total_col = cols[:, ny : ny + 1]
+        scales[t] = weights[t] * jnp.exp(cols - total_col)
+        losses[t] = jnp.sum(weights[t] * total_col, axis=0, keepdims=True) - log_total[:, rg : rg + 1]
+        features[t] = jnp.transpose(xd[t][c].reshape(rg, 128))
+        if t == 0:
+            arrived(w_ref.at[1 - c], core_recv.at[1])
+        else:
+            loss_buf[c] = jnp.broadcast_to(losses[0] + losses[1], loss_buf.shape[1:])
+            go(loss_buf.at[c], loss_buf.at[c], core_send.at[4], core_recv.at[4], sibling)
 
     def own(t, offset):
         o = (y + offset) % ny
         columns = pl.ds(pl.multiple_of(o * vw, vw), vw)
-        part = e_buf[t, o].reshape(rg, vw).astype(F32)
+        rg = rgs[t]
+        part = e_buf[t][o].reshape(rg, vw).astype(F32)
         hit = iota((rg, vw), 1) == labels[t] - (vo * (vw * ny) + o * vw)
         scaled = part * scales[t][:, offset : offset + 1]
         g_logits = jnp.where(hit, scaled - weights[t], scaled).astype(BF16)
-        g_buf[c, t, o] = g_logits
-        go(g_buf.at[c, t, o], g_buf.at[c, t, o], g_send, g_recv.at[t, offset], sibling)
+        g_buf[t][c, o] = g_logits
+        go(g_buf[t].at[c, o], g_buf[t].at[c, o], g_send.at[t], g_recv.at[t, offset], sibling)
         term = nt(w_ref[:, :, columns].reshape(256, vw), g_logits)
         if offset == 0:
-            ght[t] = term
+            ght[t][...] = term
         else:
-            ght[t] += term
+            ght[t][...] += term
         grad = nn(features[t], g_logits)
         if t == 0:
             gw_ref[:, columns] = grad
@@ -487,45 +512,41 @@
 
     def others():
         for t in range(2):
-            arrived(xd.at[1 - c, t], core_recv.at[2 + t])
-        turned = [jnp.transpose(xd[1 - c, t].reshape(rg, 128)) for t in range(2)]
+            arrived(xd[t].at[1 - c], core_recv.at[2 + t])
+        turned = [jnp.transpose(xd[t][1 - c].reshape(rgs[t], 128)) for t in range(2)]
         for offset in range(ny):
             o = (y + offset) % ny
             columns = pl.ds(pl.multiple_of(o * vw, vw), vw)
             grad = gw_ref[:, columns]
             for t in range(2):
-                arrived(g_buf.at[1 - c, t, o], g_recv.at[t, offset])
-                grad += nn(turned[t], g_buf[1 - c, t, o])
+                arrived(g_buf[t].at[1 - c, o], g_recv.at[t, offset])
+                grad += nn(turned[t], g_buf[t][1 - c, o])
             gw_ref[:, columns] = grad
 
     def piece_of(t, qq):
-        return ght.at[t, pl.ds(pl.multiple_of(qq * dg, dg), dg), :]
+        return ght[t].at[pl.ds(pl.multiple_of(qq * dg, dg), dg), :]
 
     def send_pieces(t):
         def send(k, carry):
             to = (vo + k) % nch
-            go(piece_of(t, to), red.at[t, vo], r_send, r_recv.at[t], (dp, to))
+            go(piece_of(t, to), red[t].at[vo], r_send.at[t], r_recv.at[t], (dp, to))
             return carry
 
         lax.fori_loop(1, nch, send, 0)
-        red[t, vo] = piece_of(t, vo)[...]
+        red[t][vo] = piece_of(t, vo)[...]
 
     def add_pieces(t):
-        arrived(red.at[t, 0 : nch - 1], r_recv.at[t])
-        return nn(jnp.sum(red[t], axis=0).astype(BF16), qun[t])
+        arrived(red[t].at[0 : nch - 1], r_recv.at[t])
+        return nn(jnp.sum(red[t][...], axis=0).astype(BF16), qun[t][...])
 
     softmax_part(0)
-    e_rings[0][1](0)
-    arrived(xg.at[1, 0 : (nx - 1) * nz], xf_sem.at[1])
-    softmax_part(1)
-    send_stats()
-    e_rings[1][1](0)
     arrival = [sorted({ny - 1 - s, 1 + s}) for s in range(e_last + 1)]
     ready = {0: [0], 1: [0]}
 
     def spread(t, step):
-        e_rings[t][2](step)
-        ready[t] += arrival[step]
+        if step <= e_last:
+            e_rings[t][2](step)
+            ready[t] += arrival[step]
 
     def work(t, count):
         for _ in range(min(count, len(ready[t]))):
@@ -534,20 +555,25 @@
             if offset == ny // 2:
                 send_pieces(t)
 
+    rows_come(3)
+    softmax_part(1)
     spread(0, 0)
-    column_stats()
+    column_stats(0)
     spread(1, 0)
-    if e_last > 0:
-        spread(0, 1)
-    plane_stats()
-    for step in range(1, e_last + 1):
-        spread(1, step)
-        work(0, 4)
-        if step < e_last:
-            spread(0, step + 1)
-            work(0, 2)
-            work(1, 1)
+    column_stats(1)
+    spread(0, 1)
+    plane_stats(0)
+    spread(1, 1)
+    plane_stats(1)
+    work(0, 3)
+    spread(0, 2)
+    work(0, 2)
+    spread(1, 2)
+    work(1, 3)
+    spread(0, 3)
     work(0, ny)
+    work(1, ny)
+    spread(1, 3)
     work(1, ny)
     others()
     gw_copy = pltpu.make_async_copy(gw_ref, gw_hbm, out_sem)
@@ -579,18 +605,18 @@
     gone(wc.at[0:ny], wf_sem.at[0])
     gone(blocks.at[c], core_send.at[0])
     gone(w_ref.at[c], core_send.at[1])
+    gone(loss_buf.at[c], core_send.at[4])
+    gone(xg[1].at[0 : nx - 1], x_sem.at[0])
+    gone(xg[1].at[0 : (nz - 1) * nx], zr_send)
+    gone(xg[0].at[0 : nz - 1], zu_send)
+    gone(xg[0].at[0 : (nx - 1) * nz], xf_sem.at[0])
     for t in range(2):
-        gone(xd.at[c, t], core_send.at[2 + t])
-        gone(e_buf.at[t, 0 : ny - 1], e_send.at[t])
-    gone(loss_buf.at[c], core_send.at[4])
-    gone(xg.at[0, 0 : nx - 1], x_sem.at[0])
-    gone(xg.at[0, 0 : (nz - 1) * nx], zr_send)
-    gone(xg.at[1, 0 : nz - 1], zu_send)
-    gone(xg.at[1, 0 : (nx - 1) * nz], xf_sem.at[0])
-    gone(lse_y.at[0 : ny - 1], ly_sem.at[0])
-    gone(lse_xz.at[0 : nch - 1], lp_sem.at[0])
-    gone(g_buf.at[c], g_send)
-    gone(red.at[:, 0 : nch - 1], r_send)
+        gone(xd[t].at[c], core_send.at[2 + t])
+        gone(e_buf[t].at[0 : ny - 1], e_send.at[t])
+        gone(lse_y[t].at[0 : ny - 1], ly_send.at[t])
+        gone(lse_xz[t].at[0 : nch - 1], lp_send.at[t])
+        gone(g_buf[t].at[c], g_send.at[t])
+        gone(red[t].at[0 : nch - 1], r_send.at[t])
     gw_copy.wait()
 
     @pl.when(to_self)
@@ -632,10 +658,13 @@
     vw = head_weight.shape[1] // ny
     seqs, seq = positions.shape
     slots = seqs * CAP
-    rg = LIVE // 4
-    width = -(-(rg + 1) // 128) * 128
+    rh = LIVE // 4
+    first = (7 * rh // 10 + 8) // 16 * 16
+    rps = (first, rh - first)
+    rgs = [2 * r for r in rps]
+    widths = [-(-(r + 1) // 128) * 128 for r in rgs]
     dg = 256 // nch
-    cfg = (ny, nx, nz, vw, slots, tokens, seq, ndp * tokens)
+    cfg = (ny, nx, nz, vw, slots, tokens, seq, ndp * tokens, rps)
     dma = pltpu.SemaphoreType.DMA
     scratch = [
         pltpu.SMEM(counts.shape, jnp.int32),
@@ -647,19 +676,19 @@
         pltpu.VMEM((tokens, 128), BF16),
         pltpu.VMEM((2, ny, slots + META, 128), BF16),
         pltpu.VMEM((ndp, 128, vw), BF16),
-        pltpu.VMEM((2, nch, rg // 2, 128), BF16),
-        pltpu.VMEM((2, ny, 2, rg // 2, vw), BF16),
-        pltpu.VMEM((2, 2, ny, rg, vw), BF16),
-        pltpu.VMEM((2, 2, 2, rg // 2, 128), BF16),
+        *[pltpu.VMEM((nch, r, 128), BF16) for r in rps],
+        *[pltpu.VMEM((ny, 2, r, vw), BF16) for r in rps],
+        *[pltpu.VMEM((2, ny, r, vw), BF16) for r in rgs],
+        *[pltpu.VMEM((2, 2, r, 128), BF16) for r in rps],
         pltpu.VMEM((ndp, 128), F32),
-        pltpu.VMEM((2, rg, META), F32),
-        pltpu.VMEM((2, rg, ndp * 128), BF16),
-        pltpu.VMEM((ny, 2, 1, width), F32),
-        pltpu.VMEM((nch, 2, 1, width), F32),
+        *[pltpu.VMEM((r, META), F32) for r in rgs],
+        *[pltpu.VMEM((r, ndp * 128), BF16) for r in rgs],
+        *[pltpu.VMEM((ny, 1, w), F32) for w in widths],
+        *[pltpu.VMEM((nch, 1, w), F32) for w in widths],
         pltpu.VMEM((2, 1, 128), F32),
         pltpu.VMEM(head_weight.shape, F32),
-        pltpu.VMEM((2, 256, rg), F32),
-        pltpu.VMEM((2, nch, dg, rg), F32),
+        *[pltpu.VMEM((256, r), F32) for r in rgs],
+        *[pltpu.VMEM((nch, dg, r), F32) for r in rgs],
         pltpu.VMEM((ndp, dg, 128), F32),
         pltpu.VMEM((nch // 2, dg, 128), F32),
         dma((6,)),
@@ -677,11 +706,13 @@
         dma((2,)),
         dma((2,)),
         dma((2, 2, ny // 2, 2)),
-        dma,
+        dma((2,)),
         dma((2, ny)),
         dma((2,)),
         dma((2,)),
-        dma,
+        dma((2,)),
+        dma((2,)),
+        dma((2,)),
         dma((2,)),
         dma((2,)),
         dma,

time: 100 us -> 93.9 us (0.939)
  Pallas kernels: 99.3 us -> 93.1 us
    pallas_call x1, Pallas kernels: 96.7 us -> 90.4 us  [local(): pl.pallas_call(functools.partial(kernel, cfg), out_shape=out_shape, in_sp...]
where the time goes in v3:
time: 93.9 us; the launch traced here: 93.7 us
  Pallas kernels  93.1 us (99%)
    pallas_call x1, Pallas kernels, local(): pl.pallas_call(functools.partial(kernel, cfg), out_shape=out_shape, in_sp...  90.4 us
    pallas_call x1, Pallas kernels, local(): pl.pallas_call(copies, out_shape=out_shape, in_specs=[hbm] * 3, out_specs...  2.68 us

profile of v3, /device:TPU:5, one launch (start us, length us, event | category | flops | bytes accessed | tf_op | source)
XLA Modules:
  0.0 93.7 jit_solution(2801485921822894396)
XLA Ops:
  0.6 90.4 %shard_map.85 = (f32[1,1]{1,0:T(1,128)}, bf16[64,512]{1,0:T(8,128)(2,1)}, f32[128,2048]{1,0:T(8,128)}) custom-call(s32[2]{0:T(128)} %counts_hbm.1, s32[2]{0:T(128)} %rate_hbm.1, s32[2,256]{1,0:T(2,128)} %pos_hbm.1, s32[1,512]{1,0:T(1,128)} %bitcast.3, bf16[512,2048]{1,0:T(8,128)(2,1)} %states_hbm.1, bf16[128,2048]{1,0:T(8,128)(2,1)} %w_hbm.1), custom_call_target="tpu_custom_call" | custom-call | tf_op jit(solution)/shard_map/pallas_call | solution.py:727
  91.0 2.7 %shard_map.86 = (f32[1,1]{1,0:T(1,128)}, bf16[64,512]{1,0:T(8,128)(2,1)}, f32[128,2048]{1,0:T(8,128)}) custom-call(f32[1,1]{1,0:T(1,128)} %get-tuple-element.9.loss, bf16[64,512]{1,0:T(8,128)(2,1)} %get-tuple-element.10.gh, f32[128,2048]{1,0:T(8,128)} %get-tuple-element.11.gw), custom_call_target="tpu_custom_call" | custom-call | tf_op jit(solution)/shard_map/pallas_call | solution.py:737

commit v4 on v3

--- a/solution.py
+++ b/solution.py
@@ -105,7 +105,7 @@
     u_sem,
     out_sem,
 ):
-    ny, nx, nz, vw, slots, tokens, seq, all_tokens, piece_rows = cfg
+    ny, nx, nz, vw, tokens, seq, all_tokens, piece_rows = cfg
     ndp, nch = 2 * ny, nx * nz
     xg, e_buf, g_buf, xd = (xg_0, xg_1), (e_buf_0, e_buf_1), (g_buf_0, g_buf_1), (xd_0, xd_1)
     meta, qun, ght, red = (meta_0, meta_1), (qun_0, qun_1), (ght_0, ght_1), (red_0, red_1)
@@ -232,8 +232,15 @@
     own_meta = jnp.where(row16 == 4, per_slot(counts_ref[0], counts_ref[1]), own_meta)
     loads[4].wait()
     chosen = tn(pmt[...], s_buf[...])
-    blocks[c, y, 0:slots, :] = chosen[0:slots].astype(BF16)
-    blocks[c, y, slots : slots + META, :] = own_meta.astype(BF16)
+    def in_half(shape):
+        return iota(shape, 1) // 64 == h
+
+    def turn(v):
+        return pltpu.roll(v, 64, 1)
+
+    packed = jnp.where(in_half((CAP, 128)), chosen[0:CAP], turn(chosen[CAP : 2 * CAP]))
+    blocks[c, y, 0:CAP, :] = packed.astype(BF16)
+    blocks[c, y, CAP : CAP + META, :] = own_meta.astype(BF16)
 
     n_to = (ny - 1) + 1 + (nch - 1)
     pl.semaphore_wait(barrier, n_to + ndp - jnp.where(to_self, 1, 0))
@@ -255,7 +262,7 @@
     arrived(blocks.at[1 - c], core_recv.at[0])
     go(wc.at[dp], wc.at[dp], wf_sem.at[0], wf_sem.at[1], sibling)
 
-    all_meta = blocks[:, :, slots : slots + META, :].astype(F32).reshape(ndp, META, 128)
+    all_meta = blocks[:, :, CAP : CAP + META, :].astype(F32).reshape(ndp, META, 128)
     count_rows = jnp.sum(
         jnp.where(iota((ndp, META, 128), 1) == 4, all_meta, 0.0), axis=1
     )
@@ -275,22 +282,27 @@
     bound = jnp.where(in_first, first, second)
     local_place = jnp.where(in_first, lanes, lanes - CAP)
     live = (local_place < bound) & (lanes < 2 * CAP)
-    rank_buf[...] = jnp.where(live, offset + place, -1.0)
+    ranks = jnp.where(live, offset + place, -1.0)
+    rank_buf[0] = ranks
+    rank_buf[1] = pltpu.roll(ranks, 128 - CAP, 1)
 
     def first_row(t):
         return c * (LIVE // 2) + (rgs[0] if t else 0)
 
-    def one_hot(start, rows, a):
+    def one_hot(start, rows, a, second=0):
         names = iota((rows, 128), 0) + start
-        return jnp.where(names.astype(F32) == rank_buf[a : a + 1, :], 1.0, 0.0).astype(BF16)
+        return jnp.where(names.astype(F32) == rank_buf[second, a : a + 1, :], 1.0, 0.0).astype(BF16)
 
     def own_piece(t):
-        rp = rps[t]
-        acc = jnp.zeros((rp, 128), F32)
+        rp, rg = rps[t], rgs[t]
+        parts = [jnp.zeros((rg, 128), F32)] * 2
         for a in range(ndp):
-            pick = one_hot(first_row(t) + h * rp, rp, a)
-            acc += nn(pick[:, 0:slots], blocks[a // ny, a % ny, 0:slots, :])
-        xg[t][piece] = acc.astype(BF16)
+            for i in range(2):
+                pick = one_hot(first_row(t), rg, a, i)
+                parts[i] += nn(pick[:, 0:CAP], blocks[a // ny, a % ny, 0:CAP, :])
+        upper = parts[0][0:rp] + turn(parts[1][0:rp])
+        lower = turn(parts[0][rp:rg]) + parts[1][rp:rg]
+        xg[t][piece] = jnp.where(in_half((rp, 128)), upper, lower).astype(BF16)
         return xg[t].at[piece]
 
     def metas(t):
@@ -299,7 +311,7 @@
         for a in range(ndp):
             pick = one_hot(first_row(t), rg, a)
             qun[t][:, a * 128 : (a + 1) * 128] = pick
-            total += nt(pick, blocks[a // ny, a % ny, slots : slots + META, :])
+            total += nt(pick, blocks[a // ny, a % ny, CAP : CAP + META, :])
         meta[t][...] = total
 
     def ring(n, me, block, subs, send, recv, device):
@@ -375,18 +387,13 @@
     mine = own_piece(1)
     for k in range(1, nx):
         go(mine, mine, x_sem.at[0], x_sem.at[1], peer_x((x + k) % nx))
+    take(z_near, nz, pass_on)
     arrived(xg[1].at[0 : nx - 1], x_sem.at[1])
     x_start(0)
-    take(z_near, 4, pass_on)
+    metas(0)
+    take(w_near, 4, w_arrive)
+    rows_come(0)
     metas(1)
-    rows_come(0)
-    take(z_near, 2, pass_on)
-    take(w_near, 2, w_arrive)
-    rows_come(1)
-    take(z_near, nz, pass_on)
-    metas(0)
-    take(w_near, 2, w_arrive)
-    rows_come(2)
     take(w_near, ny, w_arrive)
     go(w_ref.at[c], w_ref.at[c], core_send.at[1], core_recv.at[1], sibling)
     arrived(xg[0].at[0 : (nx - 1) * nz], xf_sem.at[1])
@@ -414,11 +421,18 @@
     ]
     e_last = e_rings[0][0]
 
+    def rows_of(pair):
+        first, second = pair[0].astype(F32), pair[1].astype(F32)
+        low = iota(first.shape, 1) < 64
+        upper = jnp.where(low, first, second)
+        lower = turn(jnp.where(low, second, first))
+        return jnp.concatenate([upper, lower], axis=0).astype(BF16)
+
     def softmax_part(t):
         rg, rp, width = rgs[t], rps[t], widths[t]
         logits = jnp.zeros((rg, vw), F32)
         for mm in range(0, ndp, 2):
-            rows = [xg[t][2 * (mm + i) : 2 * (mm + i) + 2].reshape(rg, 128) for i in range(2)]
+            rows = [rows_of(xg[t][2 * (mm + i) : 2 * (mm + i) + 2]) for i in range(2)]
             logits += nn(
                 jnp.concatenate(rows, axis=1), wc[mm : mm + 2].reshape(256, vw)
             )
@@ -482,7 +496,7 @@
         total_col = cols[:, ny : ny + 1]
         scales[t] = weights[t] * jnp.exp(cols - total_col)
         losses[t] = jnp.sum(weights[t] * total_col, axis=0, keepdims=True) - log_total[:, rg : rg + 1]
-        features[t] = jnp.transpose(xd[t][c].reshape(rg, 128))
+        features[t] = jnp.transpose(rows_of(xd[t][c]))
         if t == 0:
             arrived(w_ref.at[1 - c], core_recv.at[1])
         else:
@@ -513,7 +527,7 @@
     def others():
         for t in range(2):
             arrived(xd[t].at[1 - c], core_recv.at[2 + t])
-        turned = [jnp.transpose(xd[t][1 - c].reshape(rgs[t], 128)) for t in range(2)]
+        turned = [jnp.transpose(rows_of(xd[t][1 - c])) for t in range(2)]
         for offset in range(ny):
             o = (y + offset) % ny
             columns = pl.ds(pl.multiple_of(o * vw, vw), vw)
@@ -555,23 +569,26 @@
             if offset == ny // 2:
                 send_pieces(t)
 
+    rows_come(1)
+    rows_come(2)
+    spread(0, 0)
+    column_stats(0)
     rows_come(3)
     softmax_part(1)
-    spread(0, 0)
-    column_stats(0)
-    spread(1, 0)
-    column_stats(1)
     spread(0, 1)
     plane_stats(0)
-    spread(1, 1)
-    plane_stats(1)
-    work(0, 3)
+    work(0, 2)
+    spread(1, 0)
+    work(0, 1)
+    column_stats(1)
     spread(0, 2)
     work(0, 2)
-    spread(1, 2)
-    work(1, 3)
+    spread(1, 1)
     spread(0, 3)
     work(0, ny)
+    plane_stats(1)
+    work(1, 2)
+    spread(1, 2)
     work(1, ny)
     spread(1, 3)
     work(1, ny)
@@ -656,15 +673,14 @@
     ny, nx, nz = ndp // 2, NX, nch // NX
     tokens, d = states.shape
     vw = head_weight.shape[1] // ny
-    seqs, seq = positions.shape
-    slots = seqs * CAP
+    seq = positions.shape[1]
     rh = LIVE // 4
-    first = (7 * rh // 10 + 8) // 16 * 16
+    first = (rh // 2 + 8) // 16 * 16
     rps = (first, rh - first)
     rgs = [2 * r for r in rps]
     widths = [-(-(r + 1) // 128) * 128 for r in rgs]
     dg = 256 // nch
-    cfg = (ny, nx, nz, vw, slots, tokens, seq, ndp * tokens, rps)
+    cfg = (ny, nx, nz, vw, tokens, seq, ndp * tokens, rps)
     dma = pltpu.SemaphoreType.DMA
     scratch = [
         pltpu.SMEM(counts.shape, jnp.int32),
@@ -674,13 +690,13 @@
         pltpu.VMEM((2,) + head_weight.shape, BF16),
         pltpu.VMEM((tokens, 128), BF16),
         pltpu.VMEM((tokens, 128), BF16),
-        pltpu.VMEM((2, ny, slots + META, 128), BF16),
+        pltpu.VMEM((2, ny, CAP + META, 128), BF16),
         pltpu.VMEM((ndp, 128, vw), BF16),
         *[pltpu.VMEM((nch, r, 128), BF16) for r in rps],
         *[pltpu.VMEM((ny, 2, r, vw), BF16) for r in rps],
         *[pltpu.VMEM((2, ny, r, vw), BF16) for r in rgs],
         *[pltpu.VMEM((2, 2, r, 128), BF16) for r in rps],
-        pltpu.VMEM((ndp, 128), F32),
+        pltpu.VMEM((2, ndp, 128), F32),
         *[pltpu.VMEM((r, META), F32) for r in rgs],
         *[pltpu.VMEM((r, ndp * 128), BF16) for r in rgs],
         *[pltpu.VMEM((ny, 1, w), F32) for w in widths],

time: 93.9 us -> 87.8 us (0.935)
  Pallas kernels: 93.1 us -> 87 us
    pallas_call x1, Pallas kernels: 90.4 us -> 84.3 us  [local(): pl.pallas_call(functools.partial(kernel, cfg), out_shape=out_shape, in_sp...]
where the time goes in v4:
time: 87.8 us; the launch traced here: 87.6 us
  Pallas kernels  87 us (99%)
    pallas_call x1, Pallas kernels, local(): pl.pallas_call(functools.partial(kernel, cfg), out_shape=out_shape, in_sp...  84.3 us
    pallas_call x1, Pallas kernels, local(): pl.pallas_call(copies, out_shape=out_shape, in_specs=[hbm] * 3, out_specs...  2.68 us

profile of v4, /device:TPU:5, one launch (start us, length us, event | category | flops | bytes accessed | tf_op | source)
XLA Modules:
  0.0 87.6 jit_solution(11361146426337171908)
XLA Ops:
  0.6 84.3 %shard_map.85 = (f32[1,1]{1,0:T(1,128)}, bf16[64,512]{1,0:T(8,128)(2,1)}, f32[128,2048]{1,0:T(8,128)}) custom-call(s32[2]{0:T(128)} %counts_hbm.1, s32[2]{0:T(128)} %rate_hbm.1, s32[2,256]{1,0:T(2,128)} %pos_hbm.1, s32[1,512]{1,0:T(1,128)} %bitcast.3, bf16[512,2048]{1,0:T(8,128)(2,1)} %states_hbm.1, bf16[128,2048]{1,0:T(8,128)(2,1)} %w_hbm.1), custom_call_target="tpu_custom_call" | custom-call | tf_op jit(solution)/shard_map/pallas_call | solution.py:743
  85.0 2.7 %shard_map.86 = (f32[1,1]{1,0:T(1,128)}, bf16[64,512]{1,0:T(8,128)(2,1)}, f32[128,2048]{1,0:T(8,128)}) custom-call(f32[1,1]{1,0:T(1,128)} %get-tuple-element.9.loss, bf16[64,512]{1,0:T(8,128)(2,1)} %get-tuple-element.10.gh, f32[128,2048]{1,0:T(8,128)} %get-tuple-element.11.gw), custom_call_target="tpu_custom_call" | custom-call | tf_op jit(solution)/shard_map/pallas_call | solution.py:753

commit v5 on v4

--- a/solution.py
+++ b/solution.py
@@ -387,9 +387,10 @@
     mine = own_piece(1)
     for k in range(1, nx):
         go(mine, mine, x_sem.at[0], x_sem.at[1], peer_x((x + k) % nx))
-    take(z_near, nz, pass_on)
+    take(z_near, 4, pass_on)
     arrived(xg[1].at[0 : nx - 1], x_sem.at[1])
     x_start(0)
+    take(z_near, nz, pass_on)
     metas(0)
     take(w_near, 4, w_arrive)
     rows_come(0)

time: 87.8 us -> 86.5 us (0.985)
  Pallas kernels: 87 us -> 85.8 us
    pallas_call x1, Pallas kernels: 84.3 us -> 83.1 us  [local(): pl.pallas_call(functools.partial(kernel, cfg), out_shape=out_shape, in_sp...]
where the time goes in v5:
time: 86.5 us; the launch traced here: 86.4 us
  Pallas kernels  85.8 us (99%)
    pallas_call x1, Pallas kernels, local(): pl.pallas_call(functools.partial(kernel, cfg), out_shape=out_shape, in_sp...  83.1 us
    pallas_call x1, Pallas kernels, local(): pl.pallas_call(copies, out_shape=out_shape, in_specs=[hbm] * 3, out_specs...  2.68 us

profile of v5, /device:TPU:5, one launch (start us, length us, event | category | flops | bytes accessed | tf_op | source)
XLA Modules:
  0.0 86.4 jit_solution(4928016899552846524)
XLA Ops:
  0.6 83.1 %shard_map.85 = (f32[1,1]{1,0:T(1,128)}, bf16[64,512]{1,0:T(8,128)(2,1)}, f32[128,2048]{1,0:T(8,128)}) custom-call(s32[2]{0:T(128)} %counts_hbm.1, s32[2]{0:T(128)} %rate_hbm.1, s32[2,256]{1,0:T(2,128)} %pos_hbm.1, s32[1,512]{1,0:T(1,128)} %bitcast.3, bf16[512,2048]{1,0:T(8,128)(2,1)} %states_hbm.1, bf16[128,2048]{1,0:T(8,128)(2,1)} %w_hbm.1), custom_call_target="tpu_custom_call" | custom-call | tf_op jit(solution)/shard_map/pallas_call | solution.py:744
  83.7 2.7 %shard_map.86 = (f32[1,1]{1,0:T(1,128)}, bf16[64,512]{1,0:T(8,128)(2,1)}, f32[128,2048]{1,0:T(8,128)}) custom-call(f32[1,1]{1,0:T(1,128)} %get-tuple-element.9.loss, bf16[64,512]{1,0:T(8,128)(2,1)} %get-tuple-element.10.gh, f32[128,2048]{1,0:T(8,128)} %get-tuple-element.11.gw), custom_call_target="tpu_custom_call" | custom-call | tf_op jit(solution)/shard_map/pallas_call | solution.py:754
